TPU v7x, 256 devices: a whole 4x4x8 slice. The times are simulated.
256 devices in a mesh: dp: 8 (over x, core), expert: 32 (over y, z).
Axes of the slice: x: 4, y: 4, z: 8, core: 2. Of those that a mesh axis runs over, the one named last changes fastest.
Arguments:
- tokens: bfloat16 [32768, 7168], P(('dp', 'expert')), may hold values from -6 to 6
- out_grad: bfloat16 [32768, 7168], P(('dp', 'expert')), may hold values from -6 to 6
- expert_ids: int32 [32768, 8], P(('dp', 'expert')), may hold values from 0 to 255, as said below
- route_probs: float32 [32768, 8], P(('dp', 'expert')), may hold values from 0.1 to 1
- hosted: int32 [8], replicated, may hold values from 0 to 255, as said below
- gate_weight: bfloat16 [7168, 16384], P('dp', 'expert'), may hold values from -0.0625 to 0.0625
- up_weight: bfloat16 [7168, 16384], P('dp', 'expert'), may hold values from -0.0625 to 0.0625
- down_weight: bfloat16 [16384, 7168], P('expert', 'dp'), may hold values from -0.125 to 0.125
Outputs:
- mixed: bfloat16 [32768, 7168], P(('dp', 'expert'))
- input_grad: bfloat16 [32768, 7168], P(('dp', 'expert'))
- prob_grad: float32 [32768, 8], P(('dp', 'expert'))
- gate_grad: bfloat16 [7168, 16384], P('dp', 'expert')
- up_grad: bfloat16 [7168, 16384], P('dp', 'expert')
- down_grad: bfloat16 [16384, 7168], P('expert', 'dp')
Inputs may be any that keep to these rules, and one draw needn't show every extreme that they name: `expert_ids`: each row names 8 different experts; among the rows of one device, every hosted expert is named at most 4 times, and one hosted expert exactly 4 times on every device. `hosted`: 8 different experts, one of them expert 256 - 1.
All inputs are finite; a program needn't handle non-finite values.
Results may differ from a plain program's by a relative error of at most 0.0065.
Values may be sent and summed in bfloat16 or wider, within the bound.
A program may use at most 128 MiB of HBM per device.

v0:
```python
import jax
import jax.numpy as jnp
from jax import lax
from jax.sharding import PartitionSpec as P

CAP = 4


def slot_tables(expert_ids, hosted):
    tok_count, top_count = expert_ids.shape
    hosted_count = hosted.shape[0]
    slot_count = hosted_count * CAP
    matches = (expert_ids.reshape(tok_count * top_count, 1) == hosted[None, :]).astype(jnp.int32)
    rank_in = jnp.cumsum(matches, axis=0) - matches
    expert_pos = jnp.arange(hosted_count, dtype=jnp.int32)[None, :]
    target = (
        jnp.sum(matches * (expert_pos * CAP + rank_in), axis=1)
        + (1 - jnp.sum(matches, axis=1)) * slot_count
    )
    picked = (target[:, None] == jnp.arange(slot_count, dtype=jnp.int32)[None, :]).astype(jnp.int32)
    return picked.reshape(tok_count, top_count, slot_count)


def activate(gate_pre, up_pre, back):
    sigmoid_g = jax.nn.sigmoid(gate_pre)
    silu_gate = gate_pre * sigmoid_g
    hidden = (silu_gate * up_pre).astype(jnp.bfloat16)
    grad_gate = (back * up_pre * sigmoid_g * (1.0 + gate_pre * (1.0 - sigmoid_g))).astype(
        jnp.bfloat16
    )
    grad_up = (back * silu_gate).astype(jnp.bfloat16)
    return (hidden, grad_gate, grad_up)


def on_device(
    tokens, out_grad, expert_ids, route_probs, hosted, gate_weight, up_weight, down_weight
):
    dp_count = lax.axis_size("dp")
    expert_count = lax.axis_size("expert")
    hosted_count = hosted.shape[0]
    group_size = expert_count // hosted_count
    slot_count = hosted_count * CAP
    model_width = tokens.shape[1]
    share_width = model_width // dp_count
    row_count = dp_count * expert_count * CAP
    contract_last = (((1,), (1,)), ((), ()))
    contract_first = (((0,), (0,)), ((), ()))
    highest = lax.Precision.HIGHEST
    picked = slot_tables(expert_ids, hosted)
    chosen = jnp.sum(picked, axis=1)
    prob_table = jnp.sum(picked.astype(jnp.float32) * route_probs[:, :, None], axis=1)
    slot_prob = jnp.sum(prob_table, axis=0)
    selector = chosen.astype(jnp.bfloat16)
    tok_rows = lax.dot_general(
        selector, tokens, contract_first, preferred_element_type=jnp.float32
    ).astype(jnp.bfloat16)
    grad_rows = lax.dot_general(
        selector, out_grad, contract_first, preferred_element_type=jnp.float32
    )
    scaled = (slot_prob[:, None] * grad_rows).astype(jnp.bfloat16)
    stacked = jnp.stack([tok_rows, scaled])
    arranged = stacked.reshape(2, hosted_count, CAP, dp_count, share_width).transpose(0, 3, 1, 2, 4)
    arranged = jnp.broadcast_to(
        arranged[:, :, :, None], (2, dp_count, hosted_count, group_size, CAP, share_width)
    )
    arranged = arranged.reshape(2, dp_count, expert_count, CAP, share_width)
    received = lax.all_to_all(
        lax.all_to_all(arranged, "dp", split_axis=1, concat_axis=1, tiled=True),
        "expert",
        split_axis=2,
        concat_axis=2,
        tiled=True,
    )
    tok_in = received[0].reshape(row_count, share_width)
    grad_in = received[1].reshape(row_count, share_width)
    gate_pre = jnp.dot(tok_in, gate_weight, preferred_element_type=jnp.float32)
    up_pre = jnp.dot(tok_in, up_weight, preferred_element_type=jnp.float32)
    back = lax.dot_general(grad_in, down_weight, contract_last, preferred_element_type=jnp.float32)
    gate_pre, up_pre, back = lax.psum((gate_pre, up_pre, back), "dp")
    hidden, grad_gate, grad_up = activate(gate_pre, up_pre, back)
    out_piece = jnp.dot(hidden, down_weight, preferred_element_type=jnp.float32).astype(
        jnp.bfloat16
    )
    back_piece = lax.dot_general(
        grad_gate, gate_weight, contract_last, preferred_element_type=jnp.float32
    )
    back_piece = (
        back_piece
        + lax.dot_general(grad_up, up_weight, contract_last, preferred_element_type=jnp.float32)
    ).astype(jnp.bfloat16)
    gate_grad = lax.dot_general(
        tok_in, grad_gate, contract_first, preferred_element_type=jnp.float32
    ).astype(jnp.bfloat16)
    up_grad = lax.dot_general(
        tok_in, grad_up, contract_first, preferred_element_type=jnp.float32
    ).astype(jnp.bfloat16)
    down_grad = lax.dot_general(
        hidden, grad_in, contract_first, preferred_element_type=jnp.float32
    ).astype(jnp.bfloat16)
    outgoing = jnp.stack([out_piece, back_piece]).reshape(
        2, dp_count, expert_count, CAP, share_width
    )
    arrived = lax.all_to_all(
        lax.all_to_all(outgoing, "dp", split_axis=1, concat_axis=1, tiled=True),
        "expert",
        split_axis=2,
        concat_axis=2,
        tiled=True,
    )
    arrived = jnp.sum(
        arrived.astype(jnp.float32).reshape(
            2, dp_count, hosted_count, group_size, CAP, share_width
        ),
        axis=3,
    )
    merged = arrived.transpose(0, 2, 3, 1, 4).reshape(2, slot_count, model_width)
    expert_outs = merged[0]
    token_backs = merged[1]
    mixed = jnp.dot(prob_table, expert_outs, precision=highest).astype(jnp.bfloat16)
    input_grad = jnp.dot(chosen.astype(jnp.float32), token_backs, precision=highest).astype(
        jnp.bfloat16
    )
    scores = lax.dot_general(
        out_grad.astype(jnp.float32), expert_outs, contract_last, precision=highest
    )
    prob_grad = jnp.sum(picked.astype(jnp.float32) * scores[:, None, :], axis=2)
    return (mixed, input_grad, prob_grad, gate_grad, up_grad, down_grad)


def solution(mesh):
    return jax.shard_map(
        on_device,
        mesh=mesh,
        in_specs=(
            P(("dp", "expert"), None),
            P(("dp", "expert"), None),
            P(("dp", "expert"), None),
            P(("dp", "expert"), None),
            P(),
            P("dp", "expert"),
            P("dp", "expert"),
            P("expert", "dp"),
        ),
        out_specs=(
            P(("dp", "expert"), None),
            P(("dp", "expert"), None),
            P(("dp", "expert"), None),
            P("dp", "expert"),
            P("dp", "expert"),
            P("expert", "dp"),
        ),
        check_vma=False,
    )
```

profile of v0, /device:TPU:1, one launch (start us, length us, event | category | flops | bytes accessed | tf_op | source)
XLA Modules:
  0.0 465.9 jit_solution(6922968476871116530)
XLA Ops:
  16.2 49.3 %all_to_all.20 = bf16[2,8,32,4,896]{4,3,2,0,1:T(4,128)(2,1)S(1)} all-to-all(bf16[2,8,32,4,896]{4,3,2,0,1:T(4,128)(2,1)S(1)} %bitcast.61), channel_id=1, replica_groups=mesh['dp'=8,'expert'=32] {'dp'}, dimensions={1} | all-to-all | bytes 7340032 | tf_op jit(solution)/shard_map/all_to_all | solution.py:68
  67.4 92.0 %all_to_all.21 = bf16[2,8,32,4,896]{4,3,1,0,2:T(4,128)(2,1)S(1)} all-to-all(bf16[2,8,32,4,896]{4,3,1,0,2:T(4,128)(2,1)S(1)} %copy.52), channel_id=1, replica_groups=mesh['dp'=8,'expert'=32] {'expert'}, dimensions={2} | all-to-all | bytes 7340032 | tf_op jit(solution)/shard_map/all_to_all | solution.py:67
  159.4 2.5 fusion.12
  163.8 4.0 reshape_squeeze.7
  167.8 3.4 copy.53
  171.2 4.1 reshape_squeeze.6
  175.3 4.2 fusion.15
  179.5 2.6 fusion.14
  182.1 2.7 fusion.16
  184.8 88.1 %all-reduce.3.cloned.1.call-done = (f32[1024,512]{1,0:T(8,128)}, f32[1024,512]{1,0:T(8,128)}, f32[1024,512]{1,0:T(8,128)}) async-done(((f32[1024,512]{1,0:T(8,128)}, f32[1024,512]{1,0:T(8,128)}, f32[1024,512]{1,0:T(8,128)}), (f32[1024,512]{1,0:T(8,128)}, f32[1024,512]{1,0:T(8,128)}, f32[1024,512]{1,0:T(8,128)})) %all-reduce.3.cloned.1.call-update) | async-done | bytes 6291472 | tf_op jit(solution)/shard_map/psum | solution.py:79
  272.9 5.3 %multiply_convert_fusion.2 = (bf16[1024,512]{1,0:T(8,128)(2,1)S(1)}, bf16[1024,512]{1,0:T(8,128)(2,1)S(1)}, bf16[1024,512]{1,0:T(8,128)(2,1)}) fusion(f32[1024,512]{1,0:T(8,128)} %get-tuple-element.12, f32[1024,512]{1,0:T(8,128)} %get-tuple-element.10, f32[1024,512]{1,0:T(8,128)} %get-tuple-element.11), kind=kLoop, calls=%fused_computation.10 | loop fusion | flops 7864320 | bytes 9437184 | tf_op jit(solution)/shard_map/convert_element_type | solution.py:27
  281.7 4.2 stack.21
  285.9 2.6 fusion.17
  288.5 2.5 add_convert_fusion
  291.0 4.1 stack.22
  295.1 4.7 %pad_maximum_fusion = bf16[2,8,32,4,896]{4,3,2,0,1:T(4,128)(2,1)S(1)} fusion(bf16[1,8,32,4,896]{4,3,2,0,1:T(4,128)(2,1)} %bitcast.65, bf16[1,8,32,4,896]{4,3,2,0,1:T(4,128)(2,1)} %bitcast.64), kind=kLoop, calls=%fused_computation.6 | loop fusion | flops 1835008 | bytes 7340032 | tf_op jit(solution)/shard_map/stack | solution.py:100
  299.8 47.2 %all_to_all.22 = bf16[2,8,32,4,896]{4,3,2,0,1:T(4,128)(2,1)S(1)} all-to-all(bf16[2,8,32,4,896]{4,3,2,0,1:T(4,128)(2,1)S(1)} %pad_maximum_fusion), channel_id=1, replica_groups=mesh['dp'=8,'expert'=32] {'dp'}, dimensions={1} | all-to-all | bytes 7340032 | tf_op jit(solution)/shard_map/all_to_all | solution.py:104
  347.0 3.8 copy.57
  350.8 9.7 %all-to-all-start.3 = ((bf16[2,8,32,4,896]{4,3,1,0,2:T(4,128)(2,1)}), bf16[2,8,32,4,896]{4,3,1,0,2:T(4,128)(2,1)}, u32[]{:S(2)}, u32[]{:S(2)}) async-start(bf16[2,8,32,4,896]{4,3,1,0,2:T(4,128)(2,1)} %copy.57), calls=%async_computation.3 | async-start | bytes 7340032 | tf_op jit(solution)/shard_map/all_to_all | solution.py:103
  360.5 4.1 convolution_convert_fusion.4
  368.8 73.2 %all-to-all-done.3 = bf16[2,8,32,4,896]{4,3,1,0,2:T(4,128)(2,1)} async-done(((bf16[2,8,32,4,896]{4,3,1,0,2:T(4,128)(2,1)}), bf16[2,8,32,4,896]{4,3,1,0,2:T(4,128)(2,1)}, u32[]{:S(2)}, u32[]{:S(2)}) %all-to-all-start.3) | async-done | bytes 3670048 | tf_op jit(solution)/shard_map/all_to_all | solution.py:103
  442.0 4.3 convert_reduce_fusion
  447.5 4.2 convolution_convert_fusion
  454.9 4.2 convolution_convert_fusion.1
  (63 shorter events, 24.8 us)
Async XLA Ops:
  7.2 6.6 %copy-start = (bf16[128,7168]{1,0:T(8,128)(2,1)S(1)}, bf16[128,7168]{1,0:T(8,128)(2,1)}, u32[]{:S(2)}) copy-start(bf16[128,7168]{1,0:T(8,128)(2,1)} %param.9) | copy-start | bytes 5505028
  7.2 265.7 %all-reduce.3.cloned.1.call-start = ((), (), s32[]{:S(2)}) async-start(), calls=%async_computation.4 | async-start | bytes 12582912 | tf_op jit(solution)/shard_map/psum | solution.py:79
  12.8 1.5 copy-start.6
  171.2 4.1 copy-start.9
  175.3 4.2 copy-start.4
  175.3 4.2 copy-start.8
  179.5 2.6 copy-start.3
  179.5 2.6 copy-start.11
  272.9 6.3 %copy-start.12 = (bf16[512,896]{1,0:T(8,128)(2,1)S(1)}, bf16[512,896]{1,0:T(8,128)(2,1)}, u32[]{:S(2)}) copy-start(bf16[512,896]{1,0:T(8,128)(2,1)} %param.15) | copy-start | bytes 2752516
  278.2 1.1 copy-start.7
  285.9 2.6 copy-start.1
  285.9 2.6 copy-start.10
  350.8 91.2 %all-to-all-start.3 = ((bf16[2,8,32,4,896]{4,3,1,0,2:T(4,128)(2,1)}), bf16[2,8,32,4,896]{4,3,1,0,2:T(4,128)(2,1)}, u32[]{:S(2)}, u32[]{:S(2)}) async-start(bf16[2,8,32,4,896]{4,3,1,0,2:T(4,128)(2,1)} %copy.57), calls=%async_computation.3 | async-start | bytes 7340032 | tf_op jit(solution)/shard_map/all_to_all | solution.py:103
  360.5 4.2 copy-start.5
  364.6 2.1 copy-start.2
Sparse Core Ops, SparseCore 0:
  184.9 87.9 all-reduce.2
where the time goes:
time: 469 us; the launch traced here: 466 us
  blocking collectives  188 us (40%)
  waiting for transfers between devices  161 us (34%)
  matrix products  36.3 us (8%)
  local copies, waits for them, and re-layouts  35.8 us (8%)
  other arithmetic  20 us (4%)
  between operations  14.2 us (3%)
  starting transfers between devices  9.72 us (2%)
    all_to_all x1, blocking collectives, on_device(): lax.all_to_all(lax.all_to_all(arranged, 'dp', split_axis=1, concat_axis=1...  92 us
    psum x1, waiting for transfers between devices, on_device(): gate_pre, up_pre, back = lax.psum((gate_pre, up_pre, back), 'dp')  88.1 us
    all_to_all x1, waiting for transfers between devices, on_device(): lax.all_to_all(lax.all_to_all(outgoing, 'dp', split_axis=1, concat_axis=1...  73.2 us
    all_to_all x1, blocking collectives, on_device(): lax.all_to_all(arranged, 'dp', split_axis=1, concat_axis=1, tiled=True)  49.3 us
    all_to_all x1, blocking collectives, on_device(): lax.all_to_all(outgoing, 'dp', split_axis=1, concat_axis=1, tiled=True)  47.2 us
    all_to_all x1, starting transfers between devices, on_device(): lax.all_to_all(lax.all_to_all(outgoing, 'dp', split_axis=1, concat_axis=1...  9.68 us
  transfers between devices with their start and end apart: 2, of which 2 were waited for; matrix products, arithmetic and copies ran while one was open for 2% of the time, Pallas kernels for 0%

commit v1 on v0

v1 whole, which is shorter than its diff:
```python
import functools

import jax
import jax.numpy as jnp
from jax import lax
from jax.experimental import pallas as pl
from jax.experimental.pallas import tpu as pltpu
from jax.sharding import PartitionSpec as P

CAP = 4
BF = jnp.bfloat16
F32 = jnp.float32
MESH = pl.DeviceIdType.MESH
NT = (((1,), (1,)), ((), ()))
TN = (((0,), (0,)), ((), ()))
R, L = 0, 1


def kernel(
    width,
    ids_ref, probs_ref, hosted_ref, tokens_hbm, ograd_hbm, wg_hbm, wu_hbm, wd_hbm,
    mixed_hbm, igrad_hbm, pgrad_ref, ggrad_hbm, ugrad_hbm, dgrad_hbm,
    tokens, ograd, wg, wu, wd, mixed, igrad, ggrad, ugrad, dgrad,
    xsend, xbuf, ysend, zsrc, tokin,
    part, rs, xr1, fin, own, acts,
    outp, rbuf, zout, yback, xback, eo, perm, permt,
    insem, outsem, xs_s, xs_r, ys_s, ys_r, zs_s, zs_r,
    cx_s, cx_r, rx_s, rx_r, ag_s, ag_r,
    zb_s, zb_r, yb_s, yb_r, xb_s, xb_r,
):
    me_dp = lax.axis_index("dp")
    me_e = lax.axis_index("expert")
    x, c = lax.div(me_dp, 2), lax.rem(me_dp, 2)
    y, z = lax.div(me_e, 8), lax.rem(me_e, 8)
    myhalf = lax.div(z, 4)

    def dev(x_, c_, y_, z_):
        return (x_ * 2 + c_, y_ * 8 + z_)

    def rcopy(src, dst, ssem, rsem, where):
        return pltpu.make_async_remote_copy(
            src_ref=src, dst_ref=dst, send_sem=ssem, recv_sem=rsem,
            device_id=where, device_id_type=MESH,
        )

    other_core = dev(x, 1 - c, y, z)
    xr_dev = dev(lax.rem(x + 1, 4), c, y, z)
    xl_dev = dev(lax.rem(x + 3, 4), c, y, z)
    zr_dev = dev(x, c, y, lax.rem(z + 1, 8))
    zl_dev = dev(x, c, y, lax.rem(z + 7, 8))

    def wait_in(dst, rsem):
        rcopy(dst, dst, rsem, rsem, other_core).wait_recv()

    loads = [
        pltpu.make_async_copy(a, b, insem.at[i])
        for i, (a, b) in enumerate(
            ((tokens_hbm, tokens), (ograd_hbm, ograd), (wg_hbm, wg), (wu_hbm, wu), (wd_hbm, wd))
        )
    ]
    for load in loads:
        load.start()

    barrier = pltpu.get_barrier_semaphore()
    partners = []
    for kx in range(4):
        for kc in range(2):
            if kx or kc:
                partners.append(dev(lax.rem(x + kx, 4), lax.rem(c + kc, 2), y, z))
    for k in range(1, 4):
        partners.append(dev(x, c, lax.rem(y + k, 4), z))
    partners += [zr_dev, zl_dev]
    for partner in partners:
        pl.semaphore_signal(barrier, inc=1, device_id=partner, device_id_type=MESH)

    ids = ids_ref[...]
    probs = probs_ref[...]
    hosted = hosted_ref[...]
    matched = jnp.zeros((128, 128), F32)
    prob_at = jnp.zeros((128, 128), F32)
    for k in range(8):
        hit = (ids[:, k : k + 1] == hosted).astype(F32)
        matched = matched + hit
        prob_at = prob_at + hit * probs[:, k : k + 1]
    row = lax.broadcasted_iota(jnp.int32, (128, 128), 0)
    lane = lax.broadcasted_iota(jnp.int32, (128, 128), 1)
    before = (lane < row).astype(BF)
    rank = jnp.dot(before, matched.astype(BF), preferred_element_type=F32)
    chosen = matched * (rank == (lane & 3).astype(F32)).astype(F32)
    table = prob_at * chosen
    chosen32 = jnp.where(lane < 32, chosen, 0.0)
    select = chosen32.T[:32].astype(BF)
    slot_prob = jnp.sum(table.T[:32], axis=1, keepdims=True)

    prow = lax.broadcasted_iota(jnp.int32, (256, 256), 0)
    plane = lax.broadcasted_iota(jnp.int32, (256, 256), 1)

    def moved(q):
        return ((q >> 2) & 7) * 32 + (q >> 6) * 8 + ((q >> 5) & 1) * 4 + (q & 3)

    perm[...] = (plane == moved(prow)).astype(BF)
    permt[...] = (prow == moved(plane)).astype(BF)

    pl.semaphore_wait(barrier, len(partners))

    def x_copy(arr, kx, kc, back):
        xd, cd = lax.rem(x + kx, 4), lax.rem(c + kc, 2)
        there = xd * 2 + cd
        k = kx * 2 + kc
        if back:
            return rcopy(xback.at[arr, there], eo.at[arr, me_dp], xb_s.at[arr, k], xb_r.at[arr, k], dev(xd, cd, y, z))
        return rcopy(xsend.at[arr, there], xbuf.at[arr, me_dp], xs_s.at[arr, k], xs_r.at[arr, k], dev(xd, cd, y, z))

    def x_wait(arr, back):
        for kx in range(4):
            for kc in range(2):
                if kx or kc:
                    k = kx * 2 + kc
                    origin = lax.rem(x + 4 - kx, 4) * 2 + lax.rem(c + kc, 2)
                    if back:
                        wait_in(eo.at[arr, origin], xb_r.at[arr, k])
                    else:
                        wait_in(xbuf.at[arr, origin], xs_r.at[arr, k])

    order = ((2, 0), (2, 1), (1, 0), (3, 0), (1, 1), (3, 1), (0, 1))

    def gather_rows(arr):
        def share(index):
            columns = pl.ds(pl.multiple_of(index * width, 128), width)
            source = tokens if arr == 0 else ograd
            rows = jnp.dot(select, source[:, columns], preferred_element_type=F32)
            if arr == 1:
                rows = slot_prob * rows
            return rows.astype(BF)

        for kx, kc in order:
            there = lax.rem(x + kx, 4) * 2 + lax.rem(c + kc, 2)
            xsend[arr, there] = share(there)
            x_copy(arr, kx, kc, False).start()
        xbuf[arr, me_dp] = share(me_dp)

    def y_copy(arr, k, back):
        yd = lax.rem(y + k, 4)
        if back:
            src = zout.at[arr, :, pl.ds(pl.multiple_of(yd * 32, 32), 32)]
            return rcopy(src, yback.at[arr, y], yb_s.at[arr, k], yb_r.at[arr, k], dev(x, c, yd, z))
        dst = zsrc.at[arr, :, pl.ds(pl.multiple_of(y * 32, 32), 32)]
        return rcopy(ysend.at[arr, yd], dst, ys_s.at[arr, k], ys_r.at[arr, k], dev(x, c, yd, z))

    def y_stage(arr):
        x_wait(arr, False)
        rows = jnp.dot(perm[...], xbuf[arr].reshape(256, width), preferred_element_type=F32).astype(BF)
        ysend[arr] = rows.reshape(4, 2, 32, width)
        for k in (2, 1, 3):
            y_copy(arr, k, False).start()
        mine = pl.ds(pl.multiple_of(y * 32, 32), 32)
        zsrc[arr, :, mine] = ysend[arr, y]

    def y_wait(arr):
        for k in (1, 3, 2):
            origin = lax.rem(y + 4 - k, 4)
            wait_in(zsrc.at[arr, :, pl.ds(pl.multiple_of(origin * 32, 32), 32)], ys_r.at[arr, k])

    sign = (1, -1)
    onward = (zr_dev, zl_dev)
    backward = (zl_dev, zr_dev)
    start = (lax.rem(z + 2, 8), lax.rem(13 - z, 8))

    def place(d, half):
        return lax.rem(start[d] + 4 * half, 8)

    def origin_z(d, s):
        return lax.rem(z + 8 - sign[d] * s, 8)

    def z_send(arr, d, half, s):
        p = place(d, half)
        src = origin_z(d, s)

        @pl.when((p >= s) & (p <= 4))
        def _():
            if s == 0:
                first = lax.div(7 - p, 7)
                slot = src + first * (8 + d - src)
                rcopy(zsrc.at[arr, half], tokin.at[arr, slot], zs_s.at[arr, d, half, s], zs_r.at[arr, d, half, s + 1], onward[d]).start()
            else:
                held = src
                if s == 1:
                    second = lax.div(lax.rem(8 - p, 8), 7)
                    held = src + second * (8 + d - src)
                rcopy(tokin.at[arr, held], tokin.at[arr, src], zs_s.at[arr, d, half, s], zs_r.at[arr, d, half, s + 1], onward[d]).start()

    def z_sent(arr):
        for d in (R, L):
            for half in (0, 1):
                for s in range(5):
                    p = place(d, half)

                    @pl.when((p >= s) & (p <= 4))
                    def _():
                        rcopy(zsrc.at[arr, half], tokin.at[arr, 0], zs_s.at[arr, d, half, s], zs_r.at[arr, d, half, s + 1], onward[d]).wait_send()

    def z_step(arr, s):
        for d in (R, L):
            for half in (0, 1):
                if s > 0:
                    p = place(d, half)

                    @pl.when((p >= s) & (p <= 5))
                    def _():
                        src = origin_z(d, s)
                        slot = src
                        if s == 1:
                            second = lax.div(lax.rem(8 - p, 8), 7)
                            slot = src + second * (8 + d - src)
                        wait_in(tokin.at[arr, slot], zs_r.at[arr, d, half, s])
                if s < 5:
                    z_send(arr, d, half, s)

    def z_begin(arr):
        y_wait(arr)
        z_step(arr, 0)
        tokin[arr, z] = zsrc[arr, myhalf]

    def forward(arr):
        def body(i, carry):
            rows = tokin[arr, pl.ds(2 * i, 2)].reshape(256, width)
            if arr == 0:
                part[0, i] = jnp.dot(rows, wg[...], preferred_element_type=F32).reshape(2, 128, 512)
                part[1, i] = jnp.dot(rows, wu[...], preferred_element_type=F32).reshape(2, 128, 512)
            else:
                part[2, i] = lax.dot_general(rows, wd[...], NT, preferred_element_type=F32).reshape(2, 128, 512)
            return carry

        lax.fori_loop(0, 4, body, 0)
        c_copy(arr).start()

    kinds = (pl.ds(0, 2), pl.ds(2, 1))

    def c_copy(g):
        return rcopy(part.at[kinds[g], :, 1 - c], rs.at[kinds[g]], cx_s.at[g], cx_r.at[g], other_core)

    low, high = pl.ds(0, 256), pl.ds(256, 256)
    ahead, behind, across = lax.rem(x + 1, 4), lax.rem(x + 3, 4), lax.rem(x + 2, 4)

    def rx_copies(g):
        ks = kinds[g]
        return (
            rcopy(rs.at[ks, across, :, low], xr1.at[R, ks], rx_s.at[g, 0], rx_r.at[g, 0], xr_dev),
            rcopy(rs.at[ks, across, :, high], xr1.at[L, ks], rx_s.at[g, 1], rx_r.at[g, 1], xl_dev),
            rcopy(rs.at[ks, ahead, :, high], fin.at[0, ks], rx_s.at[g, 2], rx_r.at[g, 2], xr_dev),
            rcopy(rs.at[ks, behind, :, low], fin.at[1, ks], rx_s.at[g, 3], rx_r.at[g, 3], xl_dev),
            rcopy(xr1.at[R, ks], fin.at[2, ks], rx_s.at[g, 4], rx_r.at[g, 4], xr_dev),
            rcopy(xr1.at[L, ks], fin.at[3, ks], rx_s.at[g, 5], rx_r.at[g, 5], xl_dev),
        )

    def rs_one(g):
        c_copy(g).wait_recv()
        copies = rx_copies(g)

        def add(chunk):
            for j in ((0, 1), (2,))[g]:
                rs[j, chunk] = part[j, chunk, c] + rs[j, chunk]

        add(across)
        copies[0].start()
        copies[1].start()
        add(ahead)
        copies[2].start()
        add(behind)
        copies[3].start()
        add(x)

    def rs_two(g):
        copies = rx_copies(g)
        copies[0].wait_recv()
        for j in ((0, 1), (2,))[g]:
            xr1[R, j] = xr1[R, j] + rs[j, ahead, :, low]
        copies[4].start()
        copies[1].wait_recv()
        for j in ((0, 1), (2,))[g]:
            xr1[L, j] = xr1[L, j] + rs[j, behind, :, high]
        copies[5].start()

    def rs_end(g):
        copies = rx_copies(g)
        for k in range(2, 6):
            copies[k].wait_recv()
        for j in ((0, 1), (2,))[g]:
            own[j, :, low] = rs[j, x, :, low] + fin[1, j] + fin[2, j]
            own[j, :, high] = rs[j, x, :, high] + fin[0, j] + fin[3, j]

    def activate(g):
        gate = own[0]
        up = own[1]
        sig = jax.nn.sigmoid(gate)
        silu = gate * sig
        if g == 0:
            acts[0, me_dp] = (silu * up).astype(BF)
        else:
            back = own[2]
            acts[1, me_dp] = (back * up * sig * (1.0 + gate * (1.0 - sig))).astype(BF)
            acts[2, me_dp] = (back * silu).astype(BF)

    held = (pl.ds(0, 1), pl.ds(1, 2))

    def ag_copy(g, k):
        ks = held[g]
        before_me, after_me, far = behind * 2 + c, ahead * 2 + c, across * 2 + c
        what, where = (
            (acts.at[ks, me_dp], xr_dev),
            (acts.at[ks, me_dp], xl_dev),
            (acts.at[ks, me_dp], other_core),
            (acts.at[ks, before_me, :, low], xr_dev),
            (acts.at[ks, after_me, :, high], xl_dev),
            (acts.at[ks, before_me], other_core),
            (acts.at[ks, after_me], other_core),
            (acts.at[ks, far], other_core),
        )[k]
        return rcopy(what, what, ag_s.at[g, k], ag_r.at[g, k], where)

    def ag_wait(g, k):
        ks = held[g]
        o = 1 - c
        dst = (
            acts.at[ks, behind * 2 + c],
            acts.at[ks, ahead * 2 + c],
            acts.at[ks, x * 2 + o],
            acts.at[ks, across * 2 + c, :, low],
            acts.at[ks, across * 2 + c, :, high],
            acts.at[ks, behind * 2 + o],
            acts.at[ks, ahead * 2 + o],
            acts.at[ks, across * 2 + o],
        )[k]
        wait_in(dst, ag_r.at[g, k])

    def ag_one(g):
        for k in range(3):
            ag_copy(g, k).start()

    def ag_two(g):
        ag_wait(g, 0)
        ag_copy(g, 3).start()
        ag_copy(g, 5).start()
        ag_wait(g, 1)
        ag_copy(g, 4).start()
        ag_copy(g, 6).start()

    def ag_three(g):
        ag_wait(g, 3)
        ag_wait(g, 4)
        ag_copy(g, 7).start()
        for k in (2, 5, 6, 7):
            ag_wait(g, k)

    def partial_out(arr):
        def body(i, carry):
            two = pl.ds(2 * i, 2)
            if arr == 0:
                piece = jnp.dot(acts[0, two].reshape(256, 512), wd[...], preferred_element_type=F32)
            else:
                piece = lax.dot_general(acts[1, two].reshape(256, 512), wg[...], NT, preferred_element_type=F32)
                piece = piece + lax.dot_general(acts[2, two].reshape(256, 512), wu[...], NT, preferred_element_type=F32)
            outp[arr, two] = piece.astype(BF).reshape(2, 128, width)
            return carry

        lax.fori_loop(0, 4, body, 0)

    def zb_copy(arr, d, half, s, whole):
        src = outp.at[arr, origin_z(d, s)] if whole else rbuf.at[arr, d, half, s]
        return rcopy(src, rbuf.at[arr, d, half, s - 1], zb_s.at[arr, d, half, s], zb_r.at[arr, d, half, s - 1], backward[d])

    def zb_begin(arr):
        for s in (5, 4, 3, 2, 1):
            for d in (R, L):
                for half in (0, 1):

                    @pl.when(place(d, half) == 5)
                    def _():
                        zb_copy(arr, d, half, s, True).start()

    def zb_step(arr, s):
        for d in (R, L):
            for half in (0, 1):
                p = place(d, half)

                @pl.when((p >= s) & (p <= 4))
                def _():
                    wait_in(rbuf.at[arr, d, half, s], zb_r.at[arr, d, half, s])
                    if s > 0:

                        @pl.when(p >= 2)
                        def _():
                            total = rbuf[arr, d, half, s].astype(F32) + outp[arr, origin_z(d, s)].astype(F32)
                            rbuf[arr, d, half, s] = total.astype(BF)

                        zb_copy(arr, d, half, s, False).start()

    def zb_end(arr):
        zb_step(arr, 0)
        for half in (0, 1):
            pr, pleft = place(R, half), place(L, half)
            zout[arr, half] = jnp.zeros((128, width), BF)

            def put(*refs):
                total = refs[0][...].astype(F32)
                for ref in refs[1:]:
                    total = total + ref[...].astype(F32)
                zout[arr, half] = total.astype(BF)

            right, left, mine = rbuf.at[arr, R, half, 0], rbuf.at[arr, L, half, 0], outp.at[arr, z]

            @pl.when((myhalf == half) & (pr <= 4) & (pleft <= 4))
            def _():
                put(mine, right, left)

            @pl.when((myhalf == half) & (pr <= 4) & (pleft > 4))
            def _():
                put(mine, right)

            @pl.when((myhalf == half) & (pr > 4) & (pleft <= 4))
            def _():
                put(mine, left)

            @pl.when((myhalf != half) & (pr <= 4))
            def _():
                put(right)

            @pl.when((myhalf != half) & (pleft <= 4))
            def _():
                put(left)

        for k in (2, 1, 3):
            y_copy(arr, k, True).start()
        yback[arr, y] = zout[arr, :, pl.ds(pl.multiple_of(y * 32, 32), 32)]

    def zb_sent(arr):
        for d in (R, L):
            for half in (0, 1):
                p = place(d, half)
                for s in range(1, 6):

                    @pl.when((p >= s) & (p <= 5))
                    def _():
                        rcopy(outp.at[arr, 0], rbuf.at[arr, d, half, s - 1], zb_s.at[arr, d, half, s], zb_r.at[arr, d, half, s - 1], backward[d]).wait_send()

    def x_back(arr):
        for k in (1, 3, 2):
            origin = lax.rem(y + 4 - k, 4)
            wait_in(yback.at[arr, origin], yb_r.at[arr, k])
        rows = jnp.dot(permt[...], yback[arr].reshape(256, width), preferred_element_type=F32).astype(BF)
        xback[arr] = rows.reshape(8, 32, width)
        for kx, kc in order:
            x_copy(arr, kx, kc, True).start()
        eo[arr, me_dp] = xback[arr, me_dp]

    def weight_grad(which):
        def body(i, carry):
            tile = pl.ds(pl.multiple_of(i * 128, 128), 128)
            if which < 2:
                lhs = tokin[0, pl.ds(0, 8), :, tile].reshape(1024, 128)
                rhs = acts[1 + which].reshape(1024, 512)
                out = (ggrad, ugrad)[which]
            else:
                lhs = acts[0, :, :, tile].reshape(1024, 128)
                rhs = tokin[1, pl.ds(0, 8)].reshape(1024, width)
                out = dgrad
            out[tile, :] = lax.dot_general(lhs, rhs, TN, preferred_element_type=F32).astype(BF)
            return carry

        lax.fori_loop(0, width // 128 if which < 2 else 4, body, 0)
        stores[2 + which].start()

    stores = [
        pltpu.make_async_copy(a, b, outsem.at[i])
        for i, (a, b) in enumerate(
            ((mixed, mixed_hbm), (igrad, igrad_hbm), (ggrad, ggrad_hbm), (ugrad, ugrad_hbm), (dgrad, dgrad_hbm))
        )
    ]

    loads[0].wait()
    gather_rows(0)
    loads[1].wait()
    gather_rows(1)
    y_stage(0)
    y_stage(1)
    z_begin(0)
    for s in range(1, 6):
        z_step(0, s)
    z_begin(1)
    loads[2].wait()
    loads[3].wait()
    forward(0)
    z_step(1, 1)
    rs_one(0)
    z_step(1, 2)
    rs_two(0)
    z_step(1, 3)
    rs_end(0)
    activate(0)
    ag_one(0)
    z_step(1, 4)
    ag_two(0)
    z_step(1, 5)
    loads[4].wait()
    forward(1)
    ag_three(0)
    partial_out(0)
    zb_begin(0)
    rs_one(1)
    zb_step(0, 4)
    rs_two(1)
    zb_step(0, 3)
    rs_end(1)
    activate(1)
    ag_one(1)
    zb_step(0, 2)
    ag_two(1)
    zb_step(0, 1)
    ag_three(1)
    partial_out(1)
    zb_begin(1)
    zb_end(0)
    weight_grad(0)
    zb_step(1, 4)
    x_back(0)
    weight_grad(1)
    zb_step(1, 3)
    weight_grad(2)

    x_wait(0, True)
    big = table.astype(BF)
    rest = table - big.astype(F32)
    mid = rest.astype(BF)
    small = (rest - mid.astype(F32)).astype(BF)
    zero = jnp.zeros((128, 128), BF)
    split = jnp.where(lane < 32, big, jnp.where(lane < 64, mid, jnp.where(lane < 96, small, zero)))
    scores = jnp.zeros((128, 32), F32)
    for share in range(8):
        columns = pl.ds(share * width, width)
        outs = eo[0, share]
        mixed[:, columns] = jnp.dot(split, jnp.concatenate([outs] * 4, axis=0), preferred_element_type=F32).astype(BF)
        scores = scores + lax.dot_general(ograd[:, columns], outs, NT, preferred_element_type=F32)
        if share == 3:
            zb_step(1, 2)
    stores[0].start()
    weighted = chosen[:, :32] * scores
    lane8 = lax.broadcasted_iota(jnp.int32, (128, 8), 1)
    pgrad = jnp.zeros((128, 8), F32)
    for k in range(8):
        hit = (ids[:, k : k + 1] == hosted[:, :32]).astype(F32)
        pgrad = pgrad + jnp.where(lane8 == k, jnp.sum(hit * weighted, axis=1, keepdims=True), 0.0)
    pgrad_ref[...] = pgrad

    zb_step(1, 1)
    zb_end(1)
    x_back(1)
    x_wait(1, True)
    chosen_bf = chosen[:, :32].astype(BF)
    for share in range(8):
        igrad[:, pl.ds(share * width, width)] = jnp.dot(chosen_bf, eo[1, share], preferred_element_type=F32).astype(BF)
    stores[1].start()

    for arr in (0, 1):
        for kx, kc in order:
            x_copy(arr, kx, kc, False).wait_send()
            x_copy(arr, kx, kc, True).wait_send()
        for k in (1, 2, 3):
            y_copy(arr, k, False).wait_send()
            y_copy(arr, k, True).wait_send()
        z_sent(arr)
        zb_sent(arr)
    for g in (0, 1):
        c_copy(g).wait_send()
        for copy in rx_copies(g):
            copy.wait_send()
        for k in range(8):
            ag_copy(g, k).wait_send()
    for store in stores:
        store.wait()


def on_device(tokens, out_grad, expert_ids, route_probs, hosted, gate_weight, up_weight, down_weight):
    model_width = tokens.shape[1]
    width, hidden = gate_weight.shape
    slots = jnp.tile(jnp.repeat(hosted, CAP), 4)[None, :]
    vmem = pl.BlockSpec(memory_space=pltpu.VMEM)
    hbm = pl.BlockSpec(memory_space=pl.ANY)
    dma = pltpu.SemaphoreType.DMA
    out = pl.pallas_call(
        functools.partial(kernel, width),
        out_shape=(
            jax.ShapeDtypeStruct(tokens.shape, BF),
            jax.ShapeDtypeStruct(tokens.shape, BF),
            jax.ShapeDtypeStruct(route_probs.shape, F32),
            jax.ShapeDtypeStruct(gate_weight.shape, BF),
            jax.ShapeDtypeStruct(up_weight.shape, BF),
            jax.ShapeDtypeStruct(down_weight.shape, BF),
        ),
        in_specs=[vmem] * 3 + [hbm] * 5,
        out_specs=(hbm, hbm, vmem, hbm, hbm, hbm),
        scratch_shapes=[
            pltpu.VMEM((128, model_width), BF),
            pltpu.VMEM((128, model_width), BF),
            pltpu.VMEM((width, hidden), BF),
            pltpu.VMEM((width, hidden), BF),
            pltpu.VMEM((hidden, width), BF),
            pltpu.VMEM((128, model_width), BF),
            pltpu.VMEM((128, model_width), BF),
            pltpu.VMEM((width, hidden), BF),
            pltpu.VMEM((width, hidden), BF),
            pltpu.VMEM((hidden, width), BF),
            pltpu.VMEM((2, 8, 32, width), BF),
            pltpu.VMEM((2, 8, 32, width), BF),
            pltpu.VMEM((2, 4, 2, 32, width), BF),
            pltpu.VMEM((2, 2, 128, width), BF),
            pltpu.VMEM((2, 10, 128, width), BF),
            pltpu.VMEM((3, 4, 2, 128, hidden), F32),
            pltpu.VMEM((3, 4, 128, hidden), F32),
            pltpu.VMEM((2, 3, 128, hidden // 2), F32),
            pltpu.VMEM((4, 3, 128, hidden // 2), F32),
            pltpu.VMEM((3, 128, hidden), F32),
            pltpu.VMEM((3, 8, 128, hidden), BF),
            pltpu.VMEM((2, 8, 128, width), BF),
            pltpu.VMEM((2, 2, 2, 5, 128, width), BF),
            pltpu.VMEM((2, 2, 128, width), BF),
            pltpu.VMEM((2, 4, 2, 32, width), BF),
            pltpu.VMEM((2, 8, 32, width), BF),
            pltpu.VMEM((2, 8, 32, width), BF),
            pltpu.VMEM((256, 256), BF),
            pltpu.VMEM((256, 256), BF),
            dma((5,)), dma((5,)),
            dma((2, 8)), dma((2, 8)), dma((2, 4)), dma((2, 4)),
            dma((2, 2, 2, 5)), dma((2, 2, 2, 6)),
            dma((2,)), dma((2,)), dma((2, 6)), dma((2, 6)), dma((2, 8)), dma((2, 8)),
            dma((2, 2, 2, 6)), dma((2, 2, 2, 5)), dma((2, 4)), dma((2, 4)), dma((2, 8)), dma((2, 8)),
        ],
        compiler_params=pltpu.CompilerParams(
            collective_id=0, has_side_effects=True, vmem_limit_bytes=60 * 1024 * 1024
        ),
        cost_estimate=pl.CostEstimate(flops=9 * 2 * 1024 * 896 * 512, bytes_accessed=16_000_000, transcendentals=65536),
    )(expert_ids, route_probs, slots, tokens, out_grad, gate_weight, up_weight, down_weight)
    return tuple(out)


def solution(mesh):
    return jax.shard_map(
        on_device,
        mesh=mesh,
        in_specs=(
            P(("dp", "expert"), None),
            P(("dp", "expert"), None),
            P(("dp", "expert"), None),
            P(("dp", "expert"), None),
            P(),
            P("dp", "expert"),
            P("dp", "expert"),
            P("expert", "dp"),
        ),
        out_specs=(
            P(("dp", "expert"), None),
            P(("dp", "expert"), None),
            P(("dp", "expert"), None),
            P("dp", "expert"),
            P("dp", "expert"),
            P("expert", "dp"),
        ),
        check_vma=False,
    )
```

time: 469 us -> 200 us (0.43)
  blocking collectives: 188 us -> 0 us
  Pallas kernels: 0 us -> 184 us
  waiting for transfers between devices: 161 us -> 0 us
  matrix products: 36.3 us -> 0 us
  local copies, waits for them, and re-layouts: 35.8 us -> 13.9 us
  other arithmetic: 20 us -> 0 us
  between operations: 14.2 us -> 0.65 us
  starting transfers between devices: 9.72 us -> 0 us
    all_to_all x3 -> x0, blocking collectives: 188 us -> none  [the longest x1 92 us: on_device(): lax.all_to_all(lax.all_to_all(arranged, 'dp', split_axis=1, concat_axis=1...]
    pallas_call x0 -> x1, Pallas kernels: none -> 184 us  [on_device(): pl.pallas_call(functools.partial(kernel, width), out_shape=(jax.ShapeDtyp...]
    psum x1 -> x0, waiting for transfers between devices: 88.1 us -> none  [on_device(): gate_pre, up_pre, back = lax.psum((gate_pre, up_pre, back), 'dp')]
    all_to_all x1 -> x0, waiting for transfers between devices: 73.2 us -> none  [on_device(): lax.all_to_all(lax.all_to_all(outgoing, 'dp', split_axis=1, concat_axis=1...]
    dot_general x14 -> x0, matrix products: 36.3 us -> none  [the longest x1 4.23 us: on_device(): jnp.dot(chosen.astype(jnp.float32), token_backs, precision=highest)]
    another operation x4 -> x3, local copies, waits for them, and re-layouts: 16.4 us -> 0.69 us  [on_device(): slots = jnp.tile(jnp.repeat(hosted, CAP), 4)[None, :]]
    all_to_all x1 -> x0, starting transfers between devices: 9.68 us -> none  [on_device(): lax.all_to_all(lax.all_to_all(outgoing, 'dp', split_axis=1, concat_axis=1...]
    slice x7 -> x0, local copies, waits for them, and re-layouts: 9.3 us -> none  [the longest x2 4.42 us: on_device(): grad_in = received[1].reshape(row_count, share_width)]
  transfers between devices with their start and end apart: 2 -> 0, of which waited for: 2 -> 0; matrix products, arithmetic and copies ran while one was open for 2% -> 0% of each run, Pallas kernels for 0% -> 0%
where the time goes in v1:
time: 200 us; the launch traced here: 198 us
  Pallas kernels  184 us (92%)
  local copies, waits for them, and re-layouts  13.9 us (7%)
    pallas_call x1, Pallas kernels, on_device(): pl.pallas_call(functools.partial(kernel, width), out_shape=(jax.ShapeDtyp...  184 us
    unnamed x15, local copies, waits for them, and re-layouts  11 us

profile of v1, /device:TPU:1, one launch (start us, length us, event | category | flops | bytes accessed | tf_op | source)
XLA Modules:
  0.0 198.3 jit_solution(1826638325968673683)
XLA Ops:
  0.6 0.7 broadcast_in_dim.3
  1.4 0.1 tile.7
  1.4 0.6 broadcast_in_dim_tile.3.hosted_ref
  2.0 1.4 copy.17.ids_ref
  3.5 1.4 copy.18.probs_ref
  4.9 183.7 %shard_map.127 = (bf16[128,7168]{1,0:T(8,128)(2,1)}, bf16[128,7168]{1,0:T(8,128)(2,1)}, f32[128,8]{1,0:T(8,128)}, bf16[896,512]{1,0:T(8,128)(2,1)}, bf16[896,512]{1,0:T(8,128)(2,1)}, /*index=5*/bf16[512,896]{1,0:T(8,128)(2,1)}) custom-call(s32[128,8]{1,0:T(8,128)} %copy.17.ids_ref, f32[128,8]{1,0:T(8,128)} %copy.18.probs_ref, ...), custom_call_target="tpu_custom_call" | custom-call | flops 8455716864 | bytes 16000000 | tf_op jit(solution)/shard_map/pallas_call | solution.py:589
  188.6 1.5 copy.19
  190.1 0.0 copy-start
  190.1 3.0 %copy.25 = bf16[128,7168]{1,0:T(8,128)(2,1)} copy(bf16[128,7168]{1,0:T(8,128)(2,1)} %get-tuple-element.24) | data formatting | bytes 3670016
  193.1 0.0 copy-done
  193.1 0.0 copy-start.3
  193.1 1.2 copy.26
  194.3 0.6 copy-done.3
  194.9 0.0 copy-start.2
  194.9 0.0 copy-start.1
  194.9 0.9 copy.27
  195.8 0.6 copy-done.2
  196.4 0.9 copy.28
  197.3 0.0 copy-done.1
  197.3 0.9 copy.29
  (1 shorter events, 0.0 us)
Async XLA Ops:
  190.1 3.0 %copy-start = (bf16[128,7168]{1,0:T(8,128)(2,1)S(1)}, bf16[128,7168]{1,0:T(8,128)(2,1)}, u32[]{:S(2)}) copy-start(bf16[128,7168]{1,0:T(8,128)(2,1)} %get-tuple-element.25) | copy-start | bytes 5505028
  193.1 1.8 copy-start.3
  194.9 1.5 copy-start.2
  194.9 2.4 %copy-start.1 = (bf16[512,896]{1,0:T(8,128)(2,1)S(1)}, bf16[512,896]{1,0:T(8,128)(2,1)}, u32[]{:S(2)}) copy-start(bf16[512,896]{1,0:T(8,128)(2,1)} %get-tuple-element.29) | copy-start | bytes 2752516

commit v2 on v0

v2 whole, which is shorter than its diff:
```python
import functools

import jax
import jax.numpy as jnp
from jax import lax
from jax.experimental import pallas as pl
from jax.experimental.pallas import tpu as pltpu
from jax.sharding import PartitionSpec as P

BF = jnp.bfloat16
F32 = jnp.float32
MESH = pl.DeviceIdType.MESH
NT = (((1,), (1,)), ((), ()))
TN = (((0,), (0,)), ((), ()))
R, L = 0, 1


def kernel(
    width,
    ids_ref, probs_ref, hosted_ref, tokens_hbm, ograd_hbm, wg_hbm, wu_hbm, wd_hbm,
    mixed_hbm, pgrad_ref, ggrad_hbm, ugrad_hbm, dgrad_hbm, back_hbm, select_ref,
    tokens, ograd, wg, wu, wd, mixed, ggrad, ugrad, dgrad,
    xsend, xbuf, ysend, zsrc, tokin,
    part, rs, xr1, fin, own, acts,
    outp, rbuf, zout, yback, xback, eo, perm, permt,
    insem, outsem, xs_s, xs_r, ys_s, ys_r, zs_s, zs_r,
    cx_s, cx_r, rx_s, rx_r, ag_s, ag_r,
    zb_s, zb_r, yb_s, yb_r, xb_s, xb_r,
):
    me_dp = lax.axis_index("dp")
    me_e = lax.axis_index("expert")
    x, c = lax.div(me_dp, 2), lax.rem(me_dp, 2)
    y, z = lax.div(me_e, 8), lax.rem(me_e, 8)
    myhalf = lax.div(z, 4)

    def dev(x_, c_, y_, z_):
        return (x_ * 2 + c_, y_ * 8 + z_)

    def rcopy(src, dst, ssem, rsem, where):
        return pltpu.make_async_remote_copy(
            src_ref=src, dst_ref=dst, send_sem=ssem, recv_sem=rsem,
            device_id=where, device_id_type=MESH,
        )

    other_core = dev(x, 1 - c, y, z)
    xr_dev = dev(lax.rem(x + 1, 4), c, y, z)
    xl_dev = dev(lax.rem(x + 3, 4), c, y, z)

    def wait_in(dst, rsem):
        rcopy(dst, dst, rsem, rsem, other_core).wait_recv()

    loads = [
        pltpu.make_async_copy(a, b, insem.at[i])
        for i, (a, b) in enumerate(
            ((tokens_hbm, tokens), (ograd_hbm, ograd), (wg_hbm, wg), (wu_hbm, wu), (wd_hbm, wd))
        )
    ]
    for load in loads:
        load.start()
    stores = [
        pltpu.make_async_copy(a, b, outsem.at[i])
        for i, (a, b) in enumerate(
            ((mixed, mixed_hbm), (ggrad, ggrad_hbm), (ugrad, ugrad_hbm), (dgrad, dgrad_hbm), (eo.at[1], back_hbm))
        )
    ]

    barrier = pltpu.get_barrier_semaphore()
    partners = []
    for kx in range(4):
        for kc in range(2):
            if kx or kc:
                partners.append(dev(lax.rem(x + kx, 4), lax.rem(c + kc, 2), y, z))
    for k in range(1, 4):
        partners.append(dev(x, c, lax.rem(y + k, 4), z))
    partners += [dev(x, c, y, lax.rem(z + 1, 8)), dev(x, c, y, lax.rem(z + 7, 8))]
    for partner in partners:
        pl.semaphore_signal(barrier, inc=1, device_id=partner, device_id_type=MESH)

    row = lax.broadcasted_iota(jnp.int32, (128, 128), 0)
    lane = lax.broadcasted_iota(jnp.int32, (128, 128), 1)
    ids = ids_ref[...]
    probs = probs_ref[...]
    expert_of = (row >> 1) & 7
    hosted = jnp.zeros((128, 128), jnp.int32)
    for w in range(8):
        hosted = jnp.where(expert_of == w, hosted_ref[w], hosted)
    matched = jnp.zeros((128, 128), F32)
    prob_at = jnp.zeros((128, 128), F32)
    for k in range(8):
        hit = (ids[k : k + 1, :] == hosted).astype(F32)
        matched = matched + hit
        prob_at = prob_at + hit * probs[k : k + 1, :]
    before = (row < lane).astype(BF)
    rank = jnp.dot(matched.astype(BF), before, preferred_element_type=F32)
    cap_of = ((row >> 4) & 1) * 2 + (row & 1)
    chosen = matched * (rank == cap_of.astype(F32)).astype(F32)
    table = prob_at * chosen
    select = chosen[:32].astype(BF)
    slot_prob = jnp.sum(table[:32], axis=1, keepdims=True)
    select_ref[...] = select

    def moved(q):
        return ((q >> 1) & 7) * 16 + (q >> 5) * 4 + ((q >> 4) & 1) * 2 + (q & 1)

    perm[...] = (lane == moved(row)).astype(BF)
    permt[...] = (row == moved(lane)).astype(BF)

    def x_copy(arr, q, k, back):
        xd, cd = lax.rem(x + lax.div(k, 2), 4), lax.rem(c + lax.rem(k, 2), 2)
        there = xd * 2 + cd
        if back:
            return rcopy(xback.at[arr, q, there], eo.at[arr, me_dp, pl.ds(q * 16, 16)], xb_s.at[arr, q], xb_r.at[arr, q], dev(xd, cd, y, z))
        return rcopy(xsend.at[arr, q, there], xbuf.at[arr, q, me_dp], xs_s.at[arr, q], xs_r.at[arr, q], dev(xd, cd, y, z))

    def x_send(arr, q, back):
        def body(i, carry):
            x_copy(arr, q, lax.rem(i + 3, 7) + 1, back).start()
            return carry

        lax.fori_loop(0, 7, body, 0)

    def x_wait(arr, q, back):
        wait_in(eo.at[arr, pl.ds(0, 7), pl.ds(q * 16, 16)] if back else xbuf.at[arr, q, pl.ds(0, 7)], (xb_r if back else xs_r).at[arr, q])

    def wait_out(src, ssem):
        rcopy(src, src, ssem, ssem, other_core).wait_send()

    def gather_rows(arr):
        def body(index, carry):
            columns = pl.ds(pl.multiple_of(index * width, 128), width)
            source = tokens if arr == 0 else ograd
            rows = jnp.dot(select, source[:, columns], preferred_element_type=F32)
            if arr == 1:
                rows = slot_prob * rows
            rows = rows.astype(BF)
            for q in (0, 1):
                xsend[arr, q, index] = rows[q * 16 : q * 16 + 16]
            return carry

        lax.fori_loop(0, 8, body, 0)
        for q in (0, 1):
            xbuf[arr, q, me_dp] = xsend[arr, q, me_dp]

    def y_copy(arr, q, k, back):
        yd = lax.rem(y + k, 4)
        if back:
            src = zout.at[arr, q, :, pl.ds(pl.multiple_of(yd * 16, 16), 16)]
            return rcopy(src, yback.at[arr, q, y], yb_s.at[arr, q], yb_r.at[arr, q], dev(x, c, yd, z))
        dst = zsrc.at[arr, q, :, pl.ds(pl.multiple_of(y * 16, 16), 16)]
        return rcopy(ysend.at[arr, q, yd], dst, ys_s.at[arr, q], ys_r.at[arr, q], dev(x, c, yd, z))

    def y_stage(arr, q):
        x_wait(arr, q, False)
        rows = jnp.dot(perm[...], xbuf[arr, q].reshape(128, width), preferred_element_type=F32).astype(BF)
        ysend[arr, q] = rows.reshape(4, 2, 16, width)
        for k in (2, 1, 3):
            y_copy(arr, q, k, False).start()
        mine = pl.ds(pl.multiple_of(y * 16, 16), 16)
        zsrc[arr, q, :, mine] = ysend[arr, q, y]

    def y_wait(arr, q):
        wait_in(zsrc.at[arr, q, :, pl.ds(0, 48)], ys_r.at[arr, q])

    right0, left0 = lax.rem(z + 2, 8), lax.rem(13 - z, 8)

    def each_line(body):
        def line(i, carry):
            d, half = lax.div(i, 2), lax.rem(i, 2)
            body(d, half, lax.rem(right0 + d * (left0 + 8 - right0) + 4 * half, 8))
            return carry

        lax.fori_loop(0, 4, line, 0)

    def origin_z(d, s):
        return lax.rem(z + 8 - (1 - 2 * d) * s, 8)

    def z_dev(d, back):
        step = (2 * d - 1) if back else (1 - 2 * d)
        return dev(x, c, y, lax.rem(z + 8 + step, 8))

    def is_zero(p):
        return lax.div(7 - p, 7)

    def is_one(p):
        return is_zero(lax.rem(p + 7, 8))

    def z_send(arr, q, d, half, p, s):
        src = origin_z(d, s)
        if s == 0:
            first = is_zero(p)
            slot = src + first * (8 + d - src)
            rcopy(zsrc.at[arr, q, half], tokin.at[arr, q, slot], zs_s.at[arr, q, d, half], zs_r.at[arr, q, d, 1 - first], z_dev(d, False)).start()
        else:
            came = src + is_one(p) * (8 + d - src) if s == 1 else src
            rcopy(tokin.at[arr, q, came], tokin.at[arr, q, src], zs_s.at[arr, q, d, half], zs_r.at[arr, q, d, s + 1], z_dev(d, False)).start()

    def z_sent(arr, q):
        def body(d, half, p):
            for last in range(5):

                @pl.when(p == last)
                def _():
                    wait_out(tokin.at[arr, q, pl.ds(0, last + 1)], zs_s.at[arr, q, d, half])

        each_line(body)

    def z_step(arr, q, s):
        def body(d, half, p):
            @pl.when((p >= s) & (p <= 5))
            def _():
                src = origin_z(d, s)
                transit = is_one(p) if s == 1 else 0
                wait_in(tokin.at[arr, q, src + transit * (8 + d - src)], zs_r.at[arr, q, d, s * (1 - transit)])
                if s < 5:

                    @pl.when(p <= 4)
                    def _():
                        z_send(arr, q, d, half, p, s)

        each_line(body)

    def z_begin(arr, q):
        y_wait(arr, q)
        for far in (True, False):

            def body(d, half, p):
                @pl.when(p < 4 if far else p == 4)
                def _():
                    z_send(arr, q, d, half, p, 0)

            each_line(body)
        tokin[arr, q, z] = zsrc[arr, q, myhalf]

    def forward(arr, q):
        def body(i, carry):
            rows = tokin[arr, q, pl.ds(4 * i, 4)].reshape(256, width)
            two = pl.ds(2 * i, 2)
            if arr == 0:
                part[0, q, two] = jnp.dot(rows, wg[...], preferred_element_type=F32).reshape(2, 2, 64, 512)
                part[1, q, two] = jnp.dot(rows, wu[...], preferred_element_type=F32).reshape(2, 2, 64, 512)
            else:
                part[2, q, two] = lax.dot_general(rows, wd[...], NT, preferred_element_type=F32).reshape(2, 2, 64, 512)
            return carry

        lax.fori_loop(0, 2, body, 0)
        c_copy(arr, q).start()

    kinds = (pl.ds(0, 2), pl.ds(2, 1))
    which = ((0, 1), (2,))

    def c_copy(g, q):
        return rcopy(part.at[kinds[g], q, :, 1 - c], rs.at[kinds[g], q], cx_s.at[g, q], cx_r.at[g, q], other_core)

    low, high = pl.ds(0, 256), pl.ds(256, 256)
    ahead, behind, across = lax.rem(x + 1, 4), lax.rem(x + 3, 4), lax.rem(x + 2, 4)

    def rx_copies(g, q):
        ks = kinds[g]
        return [
            rcopy(src, dst, rx_s.at[g, q], rx_r.at[g, q, min(k, 2)], to)
            for k, (src, dst, to) in enumerate((
                (rs.at[ks, q, across, :, low], xr1.at[R, ks, q], xr_dev),
                (rs.at[ks, q, across, :, high], xr1.at[L, ks, q], xl_dev),
                (rs.at[ks, q, ahead, :, high], fin.at[0, ks, q], xr_dev),
                (rs.at[ks, q, behind, :, low], fin.at[1, ks, q], xl_dev),
                (xr1.at[R, ks, q], fin.at[2, ks, q], xr_dev),
                (xr1.at[L, ks, q], fin.at[3, ks, q], xl_dev),
            ))
        ]

    def rs_one(g, q):
        c_copy(g, q).wait_recv()
        copies = rx_copies(g, q)

        def add(chunk):
            for j in which[g]:
                rs[j, q, chunk] = part[j, q, chunk, c] + rs[j, q, chunk]

        add(across)
        copies[0].start()
        copies[1].start()
        add(ahead)
        copies[2].start()
        add(behind)
        copies[3].start()
        add(x)

    def rs_two(g, q):
        copies = rx_copies(g, q)
        copies[0].wait_recv()
        for j in which[g]:
            xr1[R, j, q] = xr1[R, j, q] + rs[j, q, ahead, :, low]
        copies[4].start()
        copies[1].wait_recv()
        for j in which[g]:
            xr1[L, j, q] = xr1[L, j, q] + rs[j, q, behind, :, high]
        copies[5].start()

    def rs_end(g, q):
        wait_in(fin.at[:, kinds[g], q], rx_r.at[g, q, 2])
        for j in which[g]:
            own[j, q, :, low] = rs[j, q, x, :, low] + fin[1, j, q] + fin[2, j, q]
            own[j, q, :, high] = rs[j, q, x, :, high] + fin[0, j, q] + fin[3, j, q]
        gate = own[0, q]
        up = own[1, q]
        sig = jax.nn.sigmoid(gate)
        silu = gate * sig
        if g == 0:
            acts[0, q, me_dp] = (silu * up).astype(BF)
        else:
            back = own[2, q]
            acts[1, q, me_dp] = (back * up * sig * (1.0 + gate * (1.0 - sig))).astype(BF)
            acts[2, q, me_dp] = (back * silu).astype(BF)
        for k in range(3):
            ag_copy(g, q, k).start()

    held = (pl.ds(0, 1), pl.ds(1, 2))

    def ag_copy(g, q, k):
        ks = held[g]
        before_me, after_me, far = behind * 2 + c, ahead * 2 + c, across * 2 + c
        what, where = (
            (acts.at[ks, q, me_dp], xr_dev),
            (acts.at[ks, q, me_dp], xl_dev),
            (acts.at[ks, q, me_dp], other_core),
            (acts.at[ks, q, before_me, :, low], xr_dev),
            (acts.at[ks, q, after_me, :, high], xl_dev),
            (acts.at[ks, q, before_me], other_core),
            (acts.at[ks, q, after_me], other_core),
            (acts.at[ks, q, far], other_core),
        )[k]
        return rcopy(what, what, ag_s.at[g, q], ag_r.at[g, q, (0, 1, 3, 2, 2, 3, 3, 3)[k]], where)

    def ag_wait(g, q, k):
        ks = held[g]
        dst = (
            acts.at[ks, q, behind * 2 + c],
            acts.at[ks, q, ahead * 2 + c],
            acts.at[ks, q, across * 2 + c],
            acts.at[ks, q, pl.ds(0, 4)],
        )[k]
        wait_in(dst, ag_r.at[g, q, k])

    def ag_two(g, q):
        ag_wait(g, q, 0)
        ag_copy(g, q, 3).start()
        ag_copy(g, q, 5).start()
        ag_wait(g, q, 1)
        ag_copy(g, q, 4).start()
        ag_copy(g, q, 6).start()

    def ag_three(g, q):
        ag_wait(g, q, 2)
        ag_copy(g, q, 7).start()
        ag_wait(g, q, 3)

    def partial_out(arr, q):
        def body(i, carry):
            four = pl.ds(4 * i, 4)
            if arr == 0:
                piece = jnp.dot(acts[0, q, four].reshape(256, 512), wd[...], preferred_element_type=F32)
            else:
                piece = lax.dot_general(acts[1, q, four].reshape(256, 512), wg[...], NT, preferred_element_type=F32)
                piece = piece + lax.dot_general(acts[2, q, four].reshape(256, 512), wu[...], NT, preferred_element_type=F32)
            outp[arr, q, four] = piece.astype(BF).reshape(4, 64, width)
            return carry

        lax.fori_loop(0, 2, body, 0)
        zb_begin(arr, q)

    def zb_copy(arr, q, d, half, p, s, whole):
        src = outp.at[arr, q, origin_z(d, s)] if whole else rbuf.at[arr, q, d, half, s]
        sem = s - 1
        if s == 1:
            sem = 5 * is_one(p)
        return rcopy(src, rbuf.at[arr, q, d, half, s - 1], zb_s.at[arr, q, d, half], zb_r.at[arr, q, d, sem], z_dev(d, True))

    def zb_begin(arr, q):
        def body(d, half, p):
            @pl.when(p == 5)
            def _():
                for s in (5, 4, 3, 2, 1):
                    zb_copy(arr, q, d, half, p, s, True).start()

        each_line(body)

    def zb_step(arr, q, s):
        def body(d, half, p):
            @pl.when((p >= s) & (p <= 4))
            def _():
                sem = s
                if s == 0:
                    sem = 5 * is_zero(p)
                wait_in(rbuf.at[arr, q, d, half, s], zb_r.at[arr, q, d, sem])
                if s > 0:

                    @pl.when(p >= 2)
                    def _():
                        total = rbuf[arr, q, d, half, s].astype(F32) + outp[arr, q, origin_z(d, s)].astype(F32)
                        rbuf[arr, q, d, half, s] = total.astype(BF)

                    zb_copy(arr, q, d, half, p, s, False).start()

        each_line(body)

    def zb_end(arr, q):
        zb_step(arr, q, 0)
        for half in (0, 1):
            pr, pleft = lax.rem(right0 + 4 * half, 8), lax.rem(left0 + 4 * half, 8)

            def put(*refs):
                total = refs[0][...].astype(F32)
                for ref in refs[1:]:
                    total = total + ref[...].astype(F32)
                zout[arr, q, half] = total.astype(BF)

            right, left, mine = rbuf.at[arr, q, R, half, 0], rbuf.at[arr, q, L, half, 0], outp.at[arr, q, z]

            @pl.when((myhalf == half) & (pr <= 4) & (pleft <= 4))
            def _():
                put(mine, right, left)

            @pl.when((myhalf == half) & (pr <= 4) & (pleft > 4))
            def _():
                put(mine, right)

            @pl.when((myhalf == half) & (pr > 4) & (pleft <= 4))
            def _():
                put(mine, left)

            @pl.when((myhalf != half) & (pr <= 4))
            def _():
                put(right)

            @pl.when((myhalf != half) & (pleft <= 4))
            def _():
                put(left)

        for k in (2, 1, 3):
            y_copy(arr, q, k, True).start()
        yback[arr, q, y] = zout[arr, q, :, pl.ds(pl.multiple_of(y * 16, 16), 16)]

    def zb_sent(arr, q):
        def body(d, half, p):
            for last in range(1, 6):

                @pl.when(p == last)
                def _():
                    wait_out(outp.at[arr, q, pl.ds(0, last)], zb_s.at[arr, q, d, half])

        each_line(body)

    def x_back(arr, q):
        wait_in(yback.at[arr, q, pl.ds(0, 3)], yb_r.at[arr, q])
        rows = jnp.dot(permt[...], yback[arr, q].reshape(128, width), preferred_element_type=F32).astype(BF)
        xback[arr, q] = rows.reshape(8, 16, width)
        x_send(arr, q, True)
        eo[arr, me_dp, pl.ds(q * 16, 16)] = xback[arr, q, me_dp]

    def weight_grad(kind):
        def body(i, carry):
            tile = pl.ds(pl.multiple_of(i * 128, 128), 128)
            total = jnp.zeros((128, 512 if kind < 2 else width), F32)
            for q in (0, 1):
                if kind < 2:
                    lhs = tokin[0, q, pl.ds(0, 8), :, tile].reshape(512, 128)
                    rhs = acts[1 + kind, q].reshape(512, 512)
                else:
                    lhs = acts[0, q, :, :, tile].reshape(512, 128)
                    rhs = tokin[1, q, pl.ds(0, 8)].reshape(512, width)
                total = total + lax.dot_general(lhs, rhs, TN, preferred_element_type=F32)
            (ggrad, ugrad, dgrad)[kind][tile, :] = total.astype(BF)
            return carry

        lax.fori_loop(0, width // 128 if kind < 2 else 4, body, 0)
        stores[1 + kind].start()

    def token_side():
        x_wait(0, 0, True)
        x_wait(0, 1, True)
        big = table.astype(BF).astype(F32)
        rest = table - big
        mid = rest.astype(BF).astype(F32)
        small = (rest - mid).astype(BF).astype(F32)
        split = jnp.where(row < 32, big, jnp.where(row < 64, mid, jnp.where(row < 96, small, 0.0))).T.astype(BF)

        def body(share, scores):
            columns = pl.ds(pl.multiple_of(share * width, 128), width)
            outs = eo[0, share]
            mixed[:, columns] = jnp.dot(split, jnp.concatenate([outs] * 4, axis=0), preferred_element_type=F32).astype(BF)
            return scores + lax.dot_general(outs, ograd[:, columns], NT, preferred_element_type=F32)

        scores = lax.fori_loop(0, 8, body, jnp.zeros((32, 128), F32))
        stores[0].start()
        weighted = chosen[:32] * scores
        for k in range(8):
            hit = (ids[k : k + 1, :] == hosted[:32]).astype(F32)
            pgrad_ref[k : k + 1, :] = jnp.sum(hit * weighted, axis=0, keepdims=True)

    def sent_mid(g, q):
        c_copy(g, q).wait_send()
        wait_out(rs.at[kinds[g], q, pl.ds(0, 3)], rx_s.at[g, q])
        wait_out(acts.at[held[g], q, pl.ds(0, 7)], ag_s.at[g, q])

    def sent_in(arr, q):
        wait_out(xsend.at[arr, q, pl.ds(0, 7)], xs_s.at[arr, q])
        wait_out(ysend.at[arr, q, pl.ds(0, 3)], ys_s.at[arr, q])
        z_sent(arr, q)

    def sent_out(arr, q):
        zb_sent(arr, q)
        wait_out(zout.at[arr, q, :, pl.ds(0, 48)], yb_s.at[arr, q])
        wait_out(xback.at[arr, q, pl.ds(0, 7)], xb_s.at[arr, q])

    T, G = 0, 1
    loads[0].wait()
    gather_rows(T)
    pl.semaphore_wait(barrier, len(partners))
    x_send(T, 0, False)
    x_send(T, 1, False)
    loads[1].wait()
    gather_rows(G)
    y_stage(T, 0)
    x_send(G, 0, False)
    x_send(G, 1, False)
    y_stage(T, 1)
    z_begin(T, 0)
    y_stage(G, 0)
    z_step(T, 0, 1)
    z_begin(T, 1)
    y_stage(G, 1)
    z_step(T, 0, 2)
    z_step(T, 1, 1)
    z_step(T, 0, 3)
    z_step(T, 1, 2)
    z_step(T, 0, 4)
    z_step(T, 1, 3)
    z_begin(G, 0)
    z_step(T, 0, 5)
    for load in loads[2:]:
        load.wait()
    forward(T, 0)
    z_step(T, 1, 4)
    z_step(G, 0, 1)
    z_step(T, 1, 5)
    z_begin(G, 1)
    forward(T, 1)
    z_step(G, 0, 2)
    rs_one(T, 0)
    z_step(G, 1, 1)
    z_step(G, 0, 3)
    rs_two(T, 0)
    rs_one(T, 1)
    z_step(G, 1, 2)
    z_step(G, 0, 4)
    rs_end(T, 0)
    rs_two(T, 1)
    z_step(G, 1, 3)
    z_step(G, 0, 5)
    forward(G, 0)
    ag_two(T, 0)
    rs_end(T, 1)
    z_step(G, 1, 4)
    ag_three(T, 0)
    partial_out(T, 0)
    ag_two(T, 1)
    rs_one(G, 0)
    z_step(G, 1, 5)
    forward(G, 1)
    zb_step(T, 0, 4)
    ag_three(T, 1)
    partial_out(T, 1)
    rs_two(G, 0)
    zb_step(T, 0, 3)
    rs_one(G, 1)
    zb_step(T, 1, 4)
    rs_end(G, 0)
    zb_step(T, 0, 2)
    rs_two(G, 1)
    zb_step(T, 1, 3)
    ag_two(G, 0)
    zb_step(T, 0, 1)
    rs_end(G, 1)
    zb_step(T, 1, 2)
    ag_three(G, 0)
    partial_out(G, 0)
    zb_end(T, 0)
    ag_two(G, 1)
    zb_step(T, 1, 1)
    zb_step(G, 0, 4)
    ag_three(G, 1)
    partial_out(G, 1)
    zb_end(T, 1)
    zb_step(G, 0, 3)
    x_back(T, 0)
    weight_grad(0)
    zb_step(G, 1, 4)
    zb_step(G, 0, 2)
    x_back(T, 1)
    weight_grad(1)
    zb_step(G, 1, 3)
    zb_step(G, 0, 1)
    weight_grad(2)
    zb_step(G, 1, 2)
    zb_end(G, 0)
    token_side()
    zb_step(G, 1, 1)
    x_back(G, 0)
    zb_end(G, 1)
    for arr in (T, G):
        for q in (0, 1):
            sent_in(arr, q)
            sent_mid(arr, q)
    for arr, q in ((T, 0), (T, 1), (G, 0)):
        sent_out(arr, q)
    x_back(G, 1)
    x_wait(G, 0, True)
    x_wait(G, 1, True)
    stores[4].start()
    sent_out(G, 1)
    for store in stores:
        store.wait()


def finish(width, mixed_in, ggrad_in, ugrad_in, dgrad_in, back, select, pgrad_in, mixed, igrad, pgrad, ggrad, ugrad, dgrad, held, gbuf, ubuf, dbuf, tile, isem, osem, tsem):
    moves = []
    for i in range(4):
        rows = pl.ds(i * 32, 32)
        moves.append((mixed_in.at[rows], held.at[rows], mixed.at[rows]))
    moves += [(ggrad_in, gbuf, ggrad), (ugrad_in, ubuf, ugrad), (dgrad_in, dbuf, dgrad)]
    come = [pltpu.make_async_copy(a, b, isem.at[i]) for i, (a, b, _) in enumerate(moves)]
    leave = [pltpu.make_async_copy(b, o, osem.at[i]) for i, (_, b, o) in enumerate(moves)]
    for move in come:
        move.start()
    pgrad[...] = pgrad_in[...]
    outs = []
    for share in range(8):
        columns = pl.ds(share * width, width)
        tile[:, columns] = lax.dot_general(select[...], back[share], TN, preferred_element_type=F32).astype(BF)
        outs.append(pltpu.make_async_copy(tile.at[:, columns], igrad.at[:, columns], tsem.at[share]))
        outs[-1].start()
        if share < 7:
            come[share].wait()
            leave[share].start()
    for out in outs + leave:
        out.wait()


def on_device(tokens, out_grad, expert_ids, route_probs, hosted, gate_weight, up_weight, down_weight):
    model_width = tokens.shape[1]
    width, hidden = gate_weight.shape
    vmem = pl.BlockSpec(memory_space=pltpu.VMEM)
    smem = pl.BlockSpec(memory_space=pltpu.SMEM)
    hbm = pl.BlockSpec(memory_space=pl.ANY)
    dma = pltpu.SemaphoreType.DMA
    row_shape = jax.ShapeDtypeStruct(tokens.shape, BF)
    side_shape = jax.ShapeDtypeStruct((8, 128), F32)
    grads = (
        jax.ShapeDtypeStruct(gate_weight.shape, BF),
        jax.ShapeDtypeStruct(up_weight.shape, BF),
        jax.ShapeDtypeStruct(down_weight.shape, BF),
    )
    mixed, pgrad, ggrad, ugrad, dgrad, back, select = pl.pallas_call(
        functools.partial(kernel, width),
        out_shape=(
            row_shape, side_shape, *grads,
            jax.ShapeDtypeStruct((8, 32, width), BF),
            jax.ShapeDtypeStruct((32, 128), BF),
        ),
        in_specs=[vmem, vmem, smem] + [hbm] * 5,
        out_specs=(hbm, vmem, hbm, hbm, hbm, hbm, vmem),
        scratch_shapes=[
            pltpu.VMEM((128, model_width), BF),
            pltpu.VMEM((128, model_width), BF),
            pltpu.VMEM((width, hidden), BF),
            pltpu.VMEM((width, hidden), BF),
            pltpu.VMEM((hidden, width), BF),
            pltpu.VMEM((128, model_width), BF),
            pltpu.VMEM((width, hidden), BF),
            pltpu.VMEM((width, hidden), BF),
            pltpu.VMEM((hidden, width), BF),
            pltpu.VMEM((2, 2, 8, 16, width), BF),
            pltpu.VMEM((2, 2, 8, 16, width), BF),
            pltpu.VMEM((2, 2, 4, 2, 16, width), BF),
            pltpu.VMEM((2, 2, 2, 64, width), BF),
            pltpu.VMEM((2, 2, 10, 64, width), BF),
            pltpu.VMEM((3, 2, 4, 2, 64, hidden), F32),
            pltpu.VMEM((3, 2, 4, 64, hidden), F32),
            pltpu.VMEM((2, 3, 2, 64, hidden // 2), F32),
            pltpu.VMEM((4, 3, 2, 64, hidden // 2), F32),
            pltpu.VMEM((3, 2, 64, hidden), F32),
            pltpu.VMEM((3, 2, 8, 64, hidden), BF),
            pltpu.VMEM((2, 2, 8, 64, width), BF),
            pltpu.VMEM((2, 2, 2, 2, 5, 64, width), BF),
            pltpu.VMEM((2, 2, 2, 64, width), BF),
            pltpu.VMEM((2, 2, 4, 2, 16, width), BF),
            pltpu.VMEM((2, 2, 8, 16, width), BF),
            pltpu.VMEM((2, 8, 32, width), BF),
            pltpu.VMEM((128, 128), BF),
            pltpu.VMEM((128, 128), BF),
            dma((5,)), dma((5,)),
            dma((2, 2)), dma((2, 2)), dma((2, 2)), dma((2, 2)),
            dma((2, 2, 2, 2)), dma((2, 2, 2, 6)),
            dma((2, 2)), dma((2, 2)), dma((2, 2)), dma((2, 2, 3)), dma((2, 2)), dma((2, 2, 4)),
            dma((2, 2, 2, 2)), dma((2, 2, 2, 6)), dma((2, 2)), dma((2, 2)), dma((2, 2)), dma((2, 2)),
        ],
        compiler_params=pltpu.CompilerParams(
            collective_id=0, has_side_effects=True, vmem_limit_bytes=60 * 1024 * 1024
        ),
        cost_estimate=pl.CostEstimate(flops=9 * 2 * 1024 * 896 * 512, bytes_accessed=16_000_000, transcendentals=65536),
    )(expert_ids.T, route_probs.T, hosted, tokens, out_grad, gate_weight, up_weight, down_weight)
    mixed, igrad, pgrad, ggrad, ugrad, dgrad = pl.pallas_call(
        functools.partial(finish, width),
        out_shape=(row_shape, row_shape, side_shape, *grads),
        in_specs=[hbm] * 4 + [vmem] * 3,
        out_specs=(hbm, hbm, vmem, hbm, hbm, hbm),
        scratch_shapes=[
            pltpu.VMEM((128, model_width), BF),
            pltpu.VMEM((width, hidden), BF),
            pltpu.VMEM((width, hidden), BF),
            pltpu.VMEM((hidden, width), BF),
            pltpu.VMEM((128, model_width), BF),
            dma((7,)), dma((7,)), dma((8,)),
        ],
        compiler_params=pltpu.CompilerParams(vmem_limit_bytes=60 * 1024 * 1024),
    )(mixed, ggrad, ugrad, dgrad, back, select, pgrad)
    return mixed, igrad, pgrad.T, ggrad, ugrad, dgrad


def solution(mesh):
    return jax.shard_map(
        on_device,
        mesh=mesh,
        in_specs=(
            P(("dp", "expert"), None),
            P(("dp", "expert"), None),
            P(("dp", "expert"), None),
            P(("dp", "expert"), None),
            P(),
            P("dp", "expert"),
            P("dp", "expert"),
            P("expert", "dp"),
        ),
        out_specs=(
            P(("dp", "expert"), None),
            P(("dp", "expert"), None),
            P(("dp", "expert"), None),
            P("dp", "expert"),
            P("dp", "expert"),
            P("expert", "dp"),
        ),
        check_vma=False,
    )
```

time: 469 us -> 172 us (0.37)
  blocking collectives: 188 us -> 0 us
  Pallas kernels: 0 us -> 172 us
  waiting for transfers between devices: 161 us -> 0 us
  matrix products: 36.3 us -> 0 us
  local copies, waits for them, and re-layouts: 35.8 us -> 0 us
  other arithmetic: 20 us -> 0 us
  between operations: 14.2 us -> 0.64 us
  starting transfers between devices: 9.72 us -> 0 us
    all_to_all x3 -> x0, blocking collectives: 188 us -> none  [the longest x1 92 us: on_device(): lax.all_to_all(lax.all_to_all(arranged, 'dp', split_axis=1, concat_axis=1...]
    pallas_call x0 -> x2, Pallas kernels: none -> 172 us  [the longest x1 165 us: on_device(): pl.pallas_call(functools.partial(kernel, width), out_shape=(row_shape, si...]
    psum x1 -> x0, waiting for transfers between devices: 88.1 us -> none  [on_device(): gate_pre, up_pre, back = lax.psum((gate_pre, up_pre, back), 'dp')]
    all_to_all x1 -> x0, waiting for transfers between devices: 73.2 us -> none  [on_device(): lax.all_to_all(lax.all_to_all(outgoing, 'dp', split_axis=1, concat_axis=1...]
    dot_general x14 -> x0, matrix products: 36.3 us -> none  [the longest x1 4.23 us: on_device(): jnp.dot(chosen.astype(jnp.float32), token_backs, precision=highest)]
    another operation x4 -> x0, local copies, waits for them, and re-layouts: 16.4 us -> none  [the longest x2 8.26 us: on_device(): jnp.stack([out_piece, back_piece])]
    all_to_all x1 -> x0, starting transfers between devices: 9.68 us -> none  [on_device(): lax.all_to_all(lax.all_to_all(outgoing, 'dp', split_axis=1, concat_axis=1...]
    slice x7 -> x0, local copies, waits for them, and re-layouts: 9.3 us -> none  [the longest x2 4.42 us: on_device(): grad_in = received[1].reshape(row_count, share_width)]
  transfers between devices with their start and end apart: 2 -> 0, of which waited for: 2 -> 0; matrix products, arithmetic and copies ran while one was open for 2% -> 0% of each run, Pallas kernels for 0% -> 0%
where the time goes in v2:
time: 172 us
  Pallas kernels  172 us (100%)
    pallas_call x1, Pallas kernels, on_device(): pl.pallas_call(functools.partial(kernel, width), out_shape=(row_shape, si...  165 us
    pallas_call x1, Pallas kernels, on_device(): pl.pallas_call(functools.partial(finish, width), out_shape=(row_shape, ro...  6.22 us

profile of v2, /device:TPU:1, one launch (start us, length us, event | category | flops | bytes accessed | tf_op | source)
XLA Modules:
  0.0 172.3 jit_solution(6593402204297573577)
XLA Ops:
  0.6 165.4 %shard_map.127 = (bf16[128,7168]{1,0:T(8,128)(2,1)}, f32[8,128]{1,0:T(8,128)}, bf16[896,512]{1,0:T(8,128)(2,1)}, bf16[896,512]{1,0:T(8,128)(2,1)}, bf16[512,896]...) custom-call(s32[8,128]{1,0:T(8,128)} %bitcast.3, f32[8,128]{1,0:T(8,128)} %bitcast.4, ...), custom_call_target="tpu_custom_call" | custom-call | flops 8455716864 | bytes 16000000 | tf_op jit(solution)/shard_map/pallas_call | solution.py:663
  166.1 6.2 %shard_map.128 = (bf16[128,7168]{1,0:T(8,128)(2,1)}, bf16[128,7168]{1,0:T(8,128)(2,1)}, f32[8,128]{1,0:T(8,128)}, bf16[896,512]{1,0:T(8,128)(2,1)}, bf16[896,512]{1,0:T(8,128)(2,1)}, /*index=5*/bf16[512,896]{1,0:T(8,128)(2,1)}) custom-call(bf16[128,7168]{1,0:T(8,128)(2,1)} %get-tuple-element.19.mixed_in, bf16[896,512]{1,0:T(8,128)(2,1)} %get-tuple-element.20.ggrad_in, ...), custom_call_target="tpu_custom_call" | custom-call | tf_op jit(solution)/shard_map/pallas_call | solution.py:712

commit v3 on v2

--- a/solution.py
+++ b/solution.py
@@ -457,7 +457,7 @@
         x_send(arr, q, True)
         eo[arr, me_dp, pl.ds(q * 16, 16)] = xback[arr, q, me_dp]
 
-    def weight_grad(kind):
+    def weight_grad(kind, piece):
         def body(i, carry):
             tile = pl.ds(pl.multiple_of(i * 128, 128), 128)
             total = jnp.zeros((128, 512 if kind < 2 else width), F32)
@@ -472,8 +472,10 @@
             (ggrad, ugrad, dgrad)[kind][tile, :] = total.astype(BF)
             return carry
 
-        lax.fori_loop(0, width // 128 if kind < 2 else 4, body, 0)
-        stores[1 + kind].start()
+        tiles = width // 128 if kind < 2 else 4
+        lax.fori_loop(piece * tiles // 3, (piece + 1) * tiles // 3, body, 0)
+        if piece == 2:
+            stores[1 + kind].start()
 
     def token_side():
         x_wait(0, 0, True)
@@ -525,95 +527,101 @@
     x_send(G, 1, False)
     y_stage(T, 1)
     z_begin(T, 0)
-    y_stage(G, 0)
     z_step(T, 0, 1)
     z_begin(T, 1)
-    y_stage(G, 1)
+    y_stage(G, 0)
     z_step(T, 0, 2)
     z_step(T, 1, 1)
     z_step(T, 0, 3)
+    z_step(T, 0, 4)
     z_step(T, 1, 2)
-    z_step(T, 0, 4)
-    z_step(T, 1, 3)
     z_begin(G, 0)
     z_step(T, 0, 5)
     for load in loads[2:]:
         load.wait()
     forward(T, 0)
+    z_step(T, 1, 3)
+    rs_one(T, 0)
+    y_stage(G, 1)
     z_step(T, 1, 4)
     z_step(G, 0, 1)
+    rs_two(T, 0)
+    z_begin(G, 1)
     z_step(T, 1, 5)
-    z_begin(G, 1)
     forward(T, 1)
+    rs_end(T, 0)
     z_step(G, 0, 2)
-    rs_one(T, 0)
+    rs_one(T, 1)
     z_step(G, 1, 1)
+    ag_two(T, 0)
+    rs_two(T, 1)
     z_step(G, 0, 3)
-    rs_two(T, 0)
-    rs_one(T, 1)
     z_step(G, 1, 2)
+    ag_three(T, 0)
+    partial_out(T, 0)
     z_step(G, 0, 4)
-    rs_end(T, 0)
-    rs_two(T, 1)
-    z_step(G, 1, 3)
+    rs_end(T, 1)
     z_step(G, 0, 5)
     forward(G, 0)
-    ag_two(T, 0)
-    rs_end(T, 1)
+    ag_two(T, 1)
+    z_step(G, 1, 3)
+    rs_one(G, 0)
+    ag_three(T, 1)
+    rs_two(G, 0)
     z_step(G, 1, 4)
-    ag_three(T, 0)
-    partial_out(T, 0)
-    ag_two(T, 1)
-    rs_one(G, 0)
+    partial_out(T, 1)
     z_step(G, 1, 5)
+    rs_end(G, 0)
     forward(G, 1)
+    ag_two(G, 0)
+    weight_grad(2, 0)
     zb_step(T, 0, 4)
-    ag_three(T, 1)
-    partial_out(T, 1)
-    rs_two(G, 0)
+    zb_step(T, 1, 4)
+    rs_one(G, 1)
+    ag_three(G, 0)
+    rs_two(G, 1)
+    partial_out(G, 0)
     zb_step(T, 0, 3)
-    rs_one(G, 1)
-    zb_step(T, 1, 4)
-    rs_end(G, 0)
+    zb_step(T, 1, 3)
+    rs_end(G, 1)
     zb_step(T, 0, 2)
-    rs_two(G, 1)
-    zb_step(T, 1, 3)
-    ag_two(G, 0)
+    zb_step(G, 0, 4)
+    weight_grad(2, 1)
+    zb_step(T, 1, 2)
+    ag_two(G, 1)
+    zb_step(G, 0, 3)
     zb_step(T, 0, 1)
-    rs_end(G, 1)
-    zb_step(T, 1, 2)
-    ag_three(G, 0)
-    partial_out(G, 0)
-    zb_end(T, 0)
-    ag_two(G, 1)
-    zb_step(T, 1, 1)
-    zb_step(G, 0, 4)
     ag_three(G, 1)
     partial_out(G, 1)
+    zb_step(T, 1, 1)
+    weight_grad(1, 0)
+    zb_end(T, 0)
+    zb_step(G, 1, 4)
+    weight_grad(0, 0)
+    zb_step(G, 0, 2)
+    zb_step(G, 1, 3)
+    weight_grad(2, 2)
+    zb_step(G, 0, 1)
+    weight_grad(0, 1)
+    zb_step(G, 1, 2)
+    x_back(T, 0)
     zb_end(T, 1)
-    zb_step(G, 0, 3)
-    x_back(T, 0)
-    weight_grad(0)
-    zb_step(G, 1, 4)
-    zb_step(G, 0, 2)
+    weight_grad(0, 2)
+    zb_step(G, 1, 1)
+    zb_end(G, 0)
+    weight_grad(1, 1)
+    weight_grad(1, 2)
     x_back(T, 1)
-    weight_grad(1)
-    zb_step(G, 1, 3)
-    zb_step(G, 0, 1)
-    weight_grad(2)
-    zb_step(G, 1, 2)
-    zb_end(G, 0)
+    zb_end(G, 1)
+    x_back(G, 0)
+    x_back(G, 1)
     token_side()
-    zb_step(G, 1, 1)
-    x_back(G, 0)
-    zb_end(G, 1)
     for arr in (T, G):
         for q in (0, 1):
             sent_in(arr, q)
             sent_mid(arr, q)
     for arr, q in ((T, 0), (T, 1), (G, 0)):
         sent_out(arr, q)
-    x_back(G, 1)
     x_wait(G, 0, True)
     x_wait(G, 1, True)
     stores[4].start()

time: 172 us -> 157 us (0.913)
  Pallas kernels: 172 us -> 157 us
    pallas_call x1, Pallas kernels: 165 us -> 150 us  [on_device(): pl.pallas_call(functools.partial(kernel, width), out_shape=(row_shape, si...]
where the time goes in v3:
time: 157 us
  Pallas kernels  157 us (100%)
    pallas_call x1, Pallas kernels, on_device(): pl.pallas_call(functools.partial(kernel, width), out_shape=(row_shape, si...  150 us
    pallas_call x1, Pallas kernels, on_device(): pl.pallas_call(functools.partial(finish, width), out_shape=(row_shape, ro...  6.22 us

profile of v3, /device:TPU:1, one launch (start us, length us, event | category | flops | bytes accessed | tf_op | source)
XLA Modules:
  0.0 157.3 jit_solution(17085818071036548990)
XLA Ops:
  0.6 150.4 %shard_map.127 = (bf16[128,7168]{1,0:T(8,128)(2,1)}, f32[8,128]{1,0:T(8,128)}, bf16[896,512]{1,0:T(8,128)(2,1)}, bf16[896,512]{1,0:T(8,128)(2,1)}, bf16[512,896]...) custom-call(s32[8,128]{1,0:T(8,128)} %bitcast.3, f32[8,128]{1,0:T(8,128)} %bitcast.4, ...), custom_call_target="tpu_custom_call" | custom-call | flops 8455716864 | bytes 16000000 | tf_op jit(solution)/shard_map/pallas_call | solution.py:671
  151.1 6.2 %shard_map.128 = (bf16[128,7168]{1,0:T(8,128)(2,1)}, bf16[128,7168]{1,0:T(8,128)(2,1)}, f32[8,128]{1,0:T(8,128)}, bf16[896,512]{1,0:T(8,128)(2,1)}, bf16[896,512]{1,0:T(8,128)(2,1)}, /*index=5*/bf16[512,896]{1,0:T(8,128)(2,1)}) custom-call(bf16[128,7168]{1,0:T(8,128)(2,1)} %get-tuple-element.19.mixed_in, bf16[896,512]{1,0:T(8,128)(2,1)} %get-tuple-element.20.ggrad_in, ...), custom_call_target="tpu_custom_call" | custom-call | tf_op jit(solution)/shard_map/pallas_call | solution.py:720

commit v4 on v3

--- a/solution.py
+++ b/solution.py
@@ -18,8 +18,8 @@
 def kernel(
     width,
     ids_ref, probs_ref, hosted_ref, tokens_hbm, ograd_hbm, wg_hbm, wu_hbm, wd_hbm,
-    mixed_hbm, pgrad_ref, ggrad_hbm, ugrad_hbm, dgrad_hbm, back_hbm, select_ref,
-    tokens, ograd, wg, wu, wd, mixed, ggrad, ugrad, dgrad,
+    split_ref, pgrad_ref, ggrad_hbm, ugrad_hbm, dgrad_hbm, eo_hbm, select_ref,
+    tokens, ograd, wg, wu, wd, ggrad, ugrad, dgrad,
     xsend, xbuf, ysend, zsrc, tokin,
     part, rs, xr1, fin, own, acts,
     outp, rbuf, zout, yback, xback, eo, perm, permt,
@@ -60,7 +60,7 @@
     stores = [
         pltpu.make_async_copy(a, b, outsem.at[i])
         for i, (a, b) in enumerate(
-            ((mixed, mixed_hbm), (ggrad, ggrad_hbm), (ugrad, ugrad_hbm), (dgrad, dgrad_hbm), (eo.at[1], back_hbm))
+            ((eo.at[0], eo_hbm.at[0]), (ggrad, ggrad_hbm), (ugrad, ugrad_hbm), (dgrad, dgrad_hbm), (eo.at[1], eo_hbm.at[1]))
         )
     ]
 
@@ -163,16 +163,15 @@
 
     right0, left0 = lax.rem(z + 2, 8), lax.rem(13 - z, 8)
 
-    def each_line(body):
-        def line(i, carry):
-            d, half = lax.div(i, 2), lax.rem(i, 2)
-            body(d, half, lax.rem(right0 + d * (left0 + 8 - right0) + 4 * half, 8))
+    def each_half(d, body):
+        def line(half, carry):
+            body(half, lax.rem((right0, left0)[d] + 4 * half, 8))
             return carry
 
-        lax.fori_loop(0, 4, line, 0)
-
-    def origin_z(d, s):
-        return lax.rem(z + 8 - (1 - 2 * d) * s, 8)
+        lax.fori_loop(0, 2, line, 0)
+
+    def slot_of(d, s):
+        return (9 + (1 - 2 * d) * s) % 8
 
     def z_dev(d, back):
         step = (2 * d - 1) if back else (1 - 2 * d)
@@ -185,65 +184,74 @@
         return is_zero(lax.rem(p + 7, 8))
 
     def z_send(arr, q, d, half, p, s):
-        src = origin_z(d, s)
+        there = slot_of(d, s + 1)
         if s == 0:
             first = is_zero(p)
-            slot = src + first * (8 + d - src)
+            slot = there + first * (8 + d - there)
             rcopy(zsrc.at[arr, q, half], tokin.at[arr, q, slot], zs_s.at[arr, q, d, half], zs_r.at[arr, q, d, 1 - first], z_dev(d, False)).start()
         else:
-            came = src + is_one(p) * (8 + d - src) if s == 1 else src
-            rcopy(tokin.at[arr, q, came], tokin.at[arr, q, src], zs_s.at[arr, q, d, half], zs_r.at[arr, q, d, s + 1], z_dev(d, False)).start()
+            came = slot_of(d, s)
+            if s == 1:
+                came = came + is_one(p) * (8 + d - came)
+            rcopy(tokin.at[arr, q, came], tokin.at[arr, q, there], zs_s.at[arr, q, d, half], zs_r.at[arr, q, d, s + 1], z_dev(d, False)).start()
 
     def z_sent(arr, q):
-        def body(d, half, p):
-            for last in range(5):
-
-                @pl.when(p == last)
-                def _():
-                    wait_out(tokin.at[arr, q, pl.ds(0, last + 1)], zs_s.at[arr, q, d, half])
-
-        each_line(body)
-
-    def z_step(arr, q, s):
-        def body(d, half, p):
+        for d in (R, L):
+
+            def body(half, p):
+                for last in range(5):
+
+                    @pl.when(p == last)
+                    def _():
+                        wait_out(tokin.at[arr, q, pl.ds(0, last + 1)], zs_s.at[arr, q, d, half])
+
+            each_half(d, body)
+
+    def z_step(arr, q, s, d):
+        def body(half, p):
             @pl.when((p >= s) & (p <= 5))
             def _():
-                src = origin_z(d, s)
-                transit = is_one(p) if s == 1 else 0
-                wait_in(tokin.at[arr, q, src + transit * (8 + d - src)], zs_r.at[arr, q, d, s * (1 - transit)])
+                slot = slot_of(d, s)
+                transit = 0
+                if s == 1:
+                    transit = is_one(p)
+                    slot = slot + transit * (8 + d - slot)
+                wait_in(tokin.at[arr, q, slot], zs_r.at[arr, q, d, s * (1 - transit)])
                 if s < 5:
 
                     @pl.when(p <= 4)
                     def _():
                         z_send(arr, q, d, half, p, s)
 
-        each_line(body)
-
-    def z_begin(arr, q):
-        y_wait(arr, q)
-        for far in (True, False):
-
-            def body(d, half, p):
+        each_half(d, body)
+
+    def z_own(arr, q, far):
+        for d in (R, L):
+
+            def body(half, p):
                 @pl.when(p < 4 if far else p == 4)
                 def _():
                     z_send(arr, q, d, half, p, 0)
 
-            each_line(body)
-        tokin[arr, q, z] = zsrc[arr, q, myhalf]
-
-    def forward(arr, q):
-        def body(i, carry):
-            rows = tokin[arr, q, pl.ds(4 * i, 4)].reshape(256, width)
-            two = pl.ds(2 * i, 2)
-            if arr == 0:
-                part[0, q, two] = jnp.dot(rows, wg[...], preferred_element_type=F32).reshape(2, 2, 64, 512)
-                part[1, q, two] = jnp.dot(rows, wu[...], preferred_element_type=F32).reshape(2, 2, 64, 512)
-            else:
-                part[2, q, two] = lax.dot_general(rows, wd[...], NT, preferred_element_type=F32).reshape(2, 2, 64, 512)
-            return carry
-
-        lax.fori_loop(0, 2, body, 0)
-        c_copy(arr, q).start()
+            each_half(d, body)
+
+    def z_far(arr, q):
+        y_wait(arr, q)
+        z_own(arr, q, True)
+        tokin[arr, q, 1] = zsrc[arr, q, myhalf]
+
+    def z_near(arr, q):
+        z_own(arr, q, False)
+
+    def forward(arr, q, part_of):
+        m = 2 * q + part_of
+        rows = tokin[arr, q, pl.ds(4 * part_of, 4)].reshape(256, width)
+        if arr == 0:
+            part[0, m] = jnp.dot(rows, wg[...], preferred_element_type=F32).reshape(4, 2, 32, 512)
+            part[1, m] = jnp.dot(rows, wu[...], preferred_element_type=F32).reshape(4, 2, 32, 512)
+        else:
+            part[2, m] = lax.dot_general(rows, wd[...], NT, preferred_element_type=F32).reshape(4, 2, 32, 512)
+        c_copy(arr, m).start()
 
     kinds = (pl.ds(0, 2), pl.ds(2, 1))
     which = ((0, 1), (2,))
@@ -349,43 +357,40 @@
         ag_copy(g, q, 4).start()
         ag_copy(g, q, 6).start()
 
-    def ag_three(g, q):
+    def ag_fwd(g, q):
         ag_wait(g, q, 2)
         ag_copy(g, q, 7).start()
-        ag_wait(g, q, 3)
-
-    def partial_out(arr, q):
-        def body(i, carry):
-            four = pl.ds(4 * i, 4)
-            if arr == 0:
-                piece = jnp.dot(acts[0, q, four].reshape(256, 512), wd[...], preferred_element_type=F32)
-            else:
-                piece = lax.dot_general(acts[1, q, four].reshape(256, 512), wg[...], NT, preferred_element_type=F32)
-                piece = piece + lax.dot_general(acts[2, q, four].reshape(256, 512), wu[...], NT, preferred_element_type=F32)
-            outp[arr, q, four] = piece.astype(BF).reshape(4, 64, width)
-            return carry
-
-        lax.fori_loop(0, 2, body, 0)
-        zb_begin(arr, q)
+
+    def partial_out(arr, q, part_of):
+        m = 2 * q + part_of
+        ag_wait(arr, m, 3)
+        if arr == 0:
+            piece = jnp.dot(acts[0, m].reshape(256, 512), wd[...], preferred_element_type=F32)
+        else:
+            piece = lax.dot_general(acts[1, m].reshape(256, 512), wg[...], NT, preferred_element_type=F32)
+            piece = piece + lax.dot_general(acts[2, m].reshape(256, 512), wu[...], NT, preferred_element_type=F32)
+        outp[arr, q, pl.ds(4 * part_of, 4)] = piece.astype(BF).reshape(4, 64, width)
 
     def zb_copy(arr, q, d, half, p, s, whole):
-        src = outp.at[arr, q, origin_z(d, s)] if whole else rbuf.at[arr, q, d, half, s]
+        src = outp.at[arr, q, slot_of(d, s)] if whole else rbuf.at[arr, q, d, half, s]
         sem = s - 1
         if s == 1:
             sem = 5 * is_one(p)
         return rcopy(src, rbuf.at[arr, q, d, half, s - 1], zb_s.at[arr, q, d, half], zb_r.at[arr, q, d, sem], z_dev(d, True))
 
     def zb_begin(arr, q):
-        def body(d, half, p):
-            @pl.when(p == 5)
-            def _():
-                for s in (5, 4, 3, 2, 1):
-                    zb_copy(arr, q, d, half, p, s, True).start()
-
-        each_line(body)
-
-    def zb_step(arr, q, s):
-        def body(d, half, p):
+        for d in (R, L):
+
+            def body(half, p):
+                @pl.when(p == 5)
+                def _():
+                    for s in (5, 4, 3, 2, 1):
+                        zb_copy(arr, q, d, half, p, s, True).start()
+
+            each_half(d, body)
+
+    def zb_step(arr, q, s, d):
+        def body(half, p):
             @pl.when((p >= s) & (p <= 4))
             def _():
                 sem = s
@@ -396,15 +401,16 @@
 
                     @pl.when(p >= 2)
                     def _():
-                        total = rbuf[arr, q, d, half, s].astype(F32) + outp[arr, q, origin_z(d, s)].astype(F32)
+                        total = rbuf[arr, q, d, half, s].astype(F32) + outp[arr, q, slot_of(d, s)].astype(F32)
                         rbuf[arr, q, d, half, s] = total.astype(BF)
 
                     zb_copy(arr, q, d, half, p, s, False).start()
 
-        each_line(body)
+        each_half(d, body)
 
     def zb_end(arr, q):
-        zb_step(arr, q, 0)
+        zb_step(arr, q, 0, R)
+        zb_step(arr, q, 0, L)
         for half in (0, 1):
             pr, pleft = lax.rem(right0 + 4 * half, 8), lax.rem(left0 + 4 * half, 8)
 
@@ -414,7 +420,7 @@
                     total = total + ref[...].astype(F32)
                 zout[arr, q, half] = total.astype(BF)
 
-            right, left, mine = rbuf.at[arr, q, R, half, 0], rbuf.at[arr, q, L, half, 0], outp.at[arr, q, z]
+            right, left, mine = rbuf.at[arr, q, R, half, 0], rbuf.at[arr, q, L, half, 0], outp.at[arr, q, 1]
 
             @pl.when((myhalf == half) & (pr <= 4) & (pleft <= 4))
             def _():
@@ -441,14 +447,16 @@
         yback[arr, q, y] = zout[arr, q, :, pl.ds(pl.multiple_of(y * 16, 16), 16)]
 
     def zb_sent(arr, q):
-        def body(d, half, p):
-            for last in range(1, 6):
-
-                @pl.when(p == last)
-                def _():
-                    wait_out(outp.at[arr, q, pl.ds(0, last)], zb_s.at[arr, q, d, half])
-
-        each_line(body)
+        for d in (R, L):
+
+            def body(half, p):
+                for last in range(1, 6):
+
+                    @pl.when(p == last)
+                    def _():
+                        wait_out(outp.at[arr, q, pl.ds(0, last)], zb_s.at[arr, q, d, half])
+
+            each_half(d, body)
 
     def x_back(arr, q):
         wait_in(yback.at[arr, q, pl.ds(0, 3)], yb_r.at[arr, q])
@@ -464,9 +472,9 @@
             for q in (0, 1):
                 if kind < 2:
                     lhs = tokin[0, q, pl.ds(0, 8), :, tile].reshape(512, 128)
-                    rhs = acts[1 + kind, q].reshape(512, 512)
+                    rhs = acts[1 + kind, pl.ds(2 * q, 2)].reshape(512, 512)
                 else:
-                    lhs = acts[0, q, :, :, tile].reshape(512, 128)
+                    lhs = acts[0, pl.ds(2 * q, 2), :, :, tile].reshape(512, 128)
                     rhs = tokin[1, q, pl.ds(0, 8)].reshape(512, width)
                 total = total + lax.dot_general(lhs, rhs, TN, preferred_element_type=F32)
             (ggrad, ugrad, dgrad)[kind][tile, :] = total.astype(BF)
@@ -480,20 +488,19 @@
     def token_side():
         x_wait(0, 0, True)
         x_wait(0, 1, True)
+        stores[0].start()
         big = table.astype(BF).astype(F32)
         rest = table - big
         mid = rest.astype(BF).astype(F32)
         small = (rest - mid).astype(BF).astype(F32)
-        split = jnp.where(row < 32, big, jnp.where(row < 64, mid, jnp.where(row < 96, small, 0.0))).T.astype(BF)
+        split_ref[...] = jnp.where(row < 32, big, jnp.where(row < 64, mid, jnp.where(row < 96, small, 0.0))).T.astype(BF)
 
         def body(share, scores):
             columns = pl.ds(pl.multiple_of(share * width, 128), width)
             outs = eo[0, share]
-            mixed[:, columns] = jnp.dot(split, jnp.concatenate([outs] * 4, axis=0), preferred_element_type=F32).astype(BF)
             return scores + lax.dot_general(outs, ograd[:, columns], NT, preferred_element_type=F32)
 
         scores = lax.fori_loop(0, 8, body, jnp.zeros((32, 128), F32))
-        stores[0].start()
         weighted = chosen[:32] * scores
         for k in range(8):
             hit = (ids[k : k + 1, :] == hosted[:32]).astype(F32)
@@ -520,106 +527,179 @@
     pl.semaphore_wait(barrier, len(partners))
     x_send(T, 0, False)
     x_send(T, 1, False)
+    y_stage(T, 0)
     loads[1].wait()
     gather_rows(G)
-    y_stage(T, 0)
-    x_send(G, 0, False)
     x_send(G, 1, False)
     y_stage(T, 1)
-    z_begin(T, 0)
-    z_step(T, 0, 1)
-    z_begin(T, 1)
+    z_far(T, 0)
+    z_near(T, 0)
+    x_send(G, 0, False)
+    z_step(T, 0, 1, R)
+    z_step(T, 0, 1, L)
+    z_far(T, 1)
+    z_near(T, 1)
+    z_step(T, 0, 2, R)
     y_stage(G, 0)
-    z_step(T, 0, 2)
-    z_step(T, 1, 1)
-    z_step(T, 0, 3)
-    z_step(T, 0, 4)
-    z_step(T, 1, 2)
-    z_begin(G, 0)
-    z_step(T, 0, 5)
+    z_step(T, 0, 2, L)
     for load in loads[2:]:
         load.wait()
-    forward(T, 0)
-    z_step(T, 1, 3)
+    forward(T, 0, 0)
+    z_step(T, 1, 1, R)
+    z_step(T, 1, 1, L)
+    z_far(G, 0)
     rs_one(T, 0)
+    z_step(T, 0, 3, R)
+    z_step(T, 0, 3, L)
     y_stage(G, 1)
-    z_step(T, 1, 4)
-    z_step(G, 0, 1)
+    z_step(T, 1, 2, L)
+    z_step(T, 1, 2, R)
     rs_two(T, 0)
-    z_begin(G, 1)
-    z_step(T, 1, 5)
-    forward(T, 1)
+    forward(T, 1, 0)
+    z_step(T, 0, 4, L)
+    z_step(T, 0, 4, R)
+    z_step(T, 0, 5, R)
+    z_near(G, 0)
+    z_far(G, 1)
+    rs_one(T, 2)
+    z_step(T, 1, 3, R)
+    z_step(T, 0, 5, L)
+    z_step(T, 1, 3, L)
+    z_near(G, 1)
+    forward(T, 0, 1)
     rs_end(T, 0)
-    z_step(G, 0, 2)
+    z_step(G, 0, 1, L)
     rs_one(T, 1)
-    z_step(G, 1, 1)
+    z_step(G, 0, 1, R)
     ag_two(T, 0)
     rs_two(T, 1)
-    z_step(G, 0, 3)
-    z_step(G, 1, 2)
-    ag_three(T, 0)
-    partial_out(T, 0)
-    z_step(G, 0, 4)
+    z_step(T, 1, 4, L)
+    z_step(T, 1, 4, R)
+    z_step(G, 1, 1, L)
+    z_step(G, 1, 1, R)
+    rs_two(T, 2)
     rs_end(T, 1)
-    z_step(G, 0, 5)
-    forward(G, 0)
+    z_step(G, 0, 2, R)
+    z_step(G, 0, 2, L)
+    ag_fwd(T, 0)
+    forward(G, 0, 0)
+    z_step(T, 1, 5, L)
+    z_step(T, 1, 5, R)
+    forward(T, 1, 1)
     ag_two(T, 1)
-    z_step(G, 1, 3)
+    partial_out(T, 0, 0)
+    rs_end(T, 2)
+    z_step(G, 1, 2, R)
     rs_one(G, 0)
-    ag_three(T, 1)
+    z_step(G, 1, 2, L)
+    ag_fwd(T, 1)
+    rs_one(T, 3)
+    z_step(G, 0, 3, R)
+    partial_out(T, 0, 1)
+    zb_begin(T, 0)
+    z_step(G, 0, 3, L)
+    forward(G, 1, 0)
+    rs_two(T, 3)
     rs_two(G, 0)
-    z_step(G, 1, 4)
-    partial_out(T, 1)
-    z_step(G, 1, 5)
+    ag_two(T, 2)
+    z_step(G, 0, 4, L)
+    z_step(G, 0, 4, R)
+    rs_one(G, 2)
+    z_step(G, 1, 3, R)
+    z_step(G, 1, 3, L)
+    rs_end(T, 3)
     rs_end(G, 0)
-    forward(G, 1)
+    z_step(G, 0, 5, L)
+    ag_fwd(T, 2)
+    z_step(G, 0, 5, R)
+    forward(G, 0, 1)
+    ag_two(T, 3)
+    rs_two(G, 2)
+    rs_one(G, 1)
+    partial_out(T, 1, 0)
+    ag_fwd(T, 3)
+    z_step(G, 1, 4, L)
+    z_step(G, 1, 4, R)
+    rs_two(G, 1)
+    partial_out(T, 1, 1)
+    zb_begin(T, 1)
+    zb_step(T, 0, 4, R)
     ag_two(G, 0)
+    rs_end(G, 1)
+    zb_step(T, 0, 4, L)
+    ag_fwd(G, 0)
+    z_step(G, 1, 5, L)
+    z_step(G, 1, 5, R)
+    rs_end(G, 2)
+    forward(G, 1, 1)
+    ag_two(G, 1)
+    zb_step(T, 1, 4, R)
     weight_grad(2, 0)
-    zb_step(T, 0, 4)
-    zb_step(T, 1, 4)
-    rs_one(G, 1)
-    ag_three(G, 0)
-    rs_two(G, 1)
-    partial_out(G, 0)
-    zb_step(T, 0, 3)
-    zb_step(T, 1, 3)
-    rs_end(G, 1)
-    zb_step(T, 0, 2)
-    zb_step(G, 0, 4)
+    rs_one(G, 3)
+    zb_step(T, 1, 4, L)
+    zb_step(T, 0, 3, R)
+    ag_fwd(G, 1)
+    rs_two(G, 3)
+    partial_out(G, 0, 0)
+    partial_out(G, 0, 1)
+    zb_begin(G, 0)
+    zb_step(T, 1, 3, L)
+    zb_step(T, 1, 3, R)
+    rs_end(G, 3)
+    ag_two(G, 2)
+    zb_step(T, 0, 3, L)
+    ag_two(G, 3)
+    zb_step(G, 0, 4, R)
+    zb_step(T, 0, 2, R)
+    zb_step(T, 0, 2, L)
+    ag_fwd(G, 2)
+    zb_step(G, 0, 4, L)
     weight_grad(2, 1)
-    zb_step(T, 1, 2)
-    ag_two(G, 1)
-    zb_step(G, 0, 3)
-    zb_step(T, 0, 1)
-    ag_three(G, 1)
-    partial_out(G, 1)
-    zb_step(T, 1, 1)
+    zb_step(T, 1, 2, R)
+    ag_fwd(G, 3)
+    partial_out(G, 1, 0)
+    zb_step(T, 1, 2, L)
+    partial_out(G, 1, 1)
+    zb_begin(G, 1)
+    zb_step(G, 0, 3, L)
+    zb_step(G, 0, 3, R)
+    zb_step(T, 0, 1, L)
+    zb_step(G, 1, 4, L)
+    zb_step(T, 0, 1, R)
+    zb_step(G, 1, 4, R)
+    zb_step(G, 0, 2, R)
+    zb_step(T, 1, 1, L)
+    weight_grad(0, 0)
     weight_grad(1, 0)
+    zb_step(G, 1, 3, R)
+    zb_step(T, 1, 1, R)
+    zb_step(G, 1, 3, L)
+    weight_grad(2, 2)
+    weight_grad(0, 1)
+    zb_step(G, 0, 2, L)
+    weight_grad(1, 1)
+    zb_step(G, 1, 2, R)
+    zb_step(G, 0, 1, R)
+    zb_step(G, 1, 2, L)
     zb_end(T, 0)
-    zb_step(G, 1, 4)
-    weight_grad(0, 0)
-    zb_step(G, 0, 2)
-    zb_step(G, 1, 3)
-    weight_grad(2, 2)
-    zb_step(G, 0, 1)
-    weight_grad(0, 1)
-    zb_step(G, 1, 2)
+    zb_step(G, 0, 1, L)
+    zb_end(T, 1)
+    zb_step(G, 1, 1, R)
+    zb_step(G, 1, 1, L)
     x_back(T, 0)
-    zb_end(T, 1)
-    weight_grad(0, 2)
-    zb_step(G, 1, 1)
     zb_end(G, 0)
-    weight_grad(1, 1)
-    weight_grad(1, 2)
     x_back(T, 1)
     zb_end(G, 1)
+    weight_grad(0, 2)
     x_back(G, 0)
+    weight_grad(1, 2)
     x_back(G, 1)
     token_side()
     for arr in (T, G):
         for q in (0, 1):
             sent_in(arr, q)
-            sent_mid(arr, q)
+        for m in range(4):
+            sent_mid(arr, m)
     for arr, q in ((T, 0), (T, 1), (G, 0)):
         sent_out(arr, q)
     x_wait(G, 0, True)
@@ -630,26 +710,31 @@
         store.wait()
 
 
-def finish(width, mixed_in, ggrad_in, ugrad_in, dgrad_in, back, select, pgrad_in, mixed, igrad, pgrad, ggrad, ugrad, dgrad, held, gbuf, ubuf, dbuf, tile, isem, osem, tsem):
-    moves = []
-    for i in range(4):
-        rows = pl.ds(i * 32, 32)
-        moves.append((mixed_in.at[rows], held.at[rows], mixed.at[rows]))
-    moves += [(ggrad_in, gbuf, ggrad), (ugrad_in, ubuf, ugrad), (dgrad_in, dbuf, dgrad)]
+def finish(width, eo_in, ggrad_in, ugrad_in, dgrad_in, split, select, pgrad_in, mixed, igrad, pgrad, ggrad, ugrad, dgrad, eo, gbuf, ubuf, dbuf, mtile, itile, esem, isem, osem, tsem):
+    rows = [pltpu.make_async_copy(eo_in.at[a, pl.ds(4 * h, 4)], eo.at[a, pl.ds(4 * h, 4)], esem.at[a, h]) for h in (0, 1) for a in (0, 1)]
+    moves = ((ggrad_in, gbuf, ggrad), (ugrad_in, ubuf, ugrad), (dgrad_in, dbuf, dgrad))
     come = [pltpu.make_async_copy(a, b, isem.at[i]) for i, (a, b, _) in enumerate(moves)]
     leave = [pltpu.make_async_copy(b, o, osem.at[i]) for i, (_, b, o) in enumerate(moves)]
-    for move in come:
+    for move in rows + come:
         move.start()
     pgrad[...] = pgrad_in[...]
     outs = []
-    for share in range(8):
-        columns = pl.ds(share * width, width)
-        tile[:, columns] = lax.dot_general(select[...], back[share], TN, preferred_element_type=F32).astype(BF)
-        outs.append(pltpu.make_async_copy(tile.at[:, columns], igrad.at[:, columns], tsem.at[share]))
-        outs[-1].start()
-        if share < 7:
-            come[share].wait()
-            leave[share].start()
+    for pair in range(4):
+        if pair % 2 == 0:
+            rows[pair].wait()
+            rows[pair + 1].wait()
+        else:
+            for k in ((0,), (1, 2))[pair // 2]:
+                come[k].wait()
+                leave[k].start()
+        for share in (2 * pair, 2 * pair + 1):
+            columns = pl.ds(share * width, width)
+            mtile[:, columns] = jnp.dot(split[...], jnp.concatenate([eo[0, share]] * 4, axis=0), preferred_element_type=F32).astype(BF)
+            itile[:, columns] = lax.dot_general(select[...], eo[1, share], TN, preferred_element_type=F32).astype(BF)
+        columns = pl.ds(2 * pair * width, 2 * width)
+        for k, (tile, to) in enumerate(((mtile, mixed), (itile, igrad))):
+            outs.append(pltpu.make_async_copy(tile.at[:, columns], to.at[:, columns], tsem.at[k, pair]))
+            outs[-1].start()
     for out in outs + leave:
         out.wait()
 
@@ -668,22 +753,21 @@
         jax.ShapeDtypeStruct(up_weight.shape, BF),
         jax.ShapeDtypeStruct(down_weight.shape, BF),
     )
-    mixed, pgrad, ggrad, ugrad, dgrad, back, select = pl.pallas_call(
+    split, pgrad, ggrad, ugrad, dgrad, eo, select = pl.pallas_call(
         functools.partial(kernel, width),
         out_shape=(
-            row_shape, side_shape, *grads,
-            jax.ShapeDtypeStruct((8, 32, width), BF),
+            jax.ShapeDtypeStruct((128, 128), BF), side_shape, *grads,
+            jax.ShapeDtypeStruct((2, 8, 32, width), BF),
             jax.ShapeDtypeStruct((32, 128), BF),
         ),
         in_specs=[vmem, vmem, smem] + [hbm] * 5,
-        out_specs=(hbm, vmem, hbm, hbm, hbm, hbm, vmem),
+        out_specs=(vmem, vmem, hbm, hbm, hbm, hbm, vmem),
         scratch_shapes=[
             pltpu.VMEM((128, model_width), BF),
             pltpu.VMEM((128, model_width), BF),
             pltpu.VMEM((width, hidden), BF),
             pltpu.VMEM((width, hidden), BF),
             pltpu.VMEM((hidden, width), BF),
-            pltpu.VMEM((128, model_width), BF),
             pltpu.VMEM((width, hidden), BF),
             pltpu.VMEM((width, hidden), BF),
             pltpu.VMEM((hidden, width), BF),
@@ -692,12 +776,12 @@
             pltpu.VMEM((2, 2, 4, 2, 16, width), BF),
             pltpu.VMEM((2, 2, 2, 64, width), BF),
             pltpu.VMEM((2, 2, 10, 64, width), BF),
-            pltpu.VMEM((3, 2, 4, 2, 64, hidden), F32),
-            pltpu.VMEM((3, 2, 4, 64, hidden), F32),
-            pltpu.VMEM((2, 3, 2, 64, hidden // 2), F32),
-            pltpu.VMEM((4, 3, 2, 64, hidden // 2), F32),
-            pltpu.VMEM((3, 2, 64, hidden), F32),
-            pltpu.VMEM((3, 2, 8, 64, hidden), BF),
+            pltpu.VMEM((3, 4, 4, 2, 32, hidden), F32),
+            pltpu.VMEM((3, 4, 4, 32, hidden), F32),
+            pltpu.VMEM((2, 3, 4, 32, hidden // 2), F32),
+            pltpu.VMEM((4, 3, 4, 32, hidden // 2), F32),
+            pltpu.VMEM((3, 4, 32, hidden), F32),
+            pltpu.VMEM((3, 4, 8, 32, hidden), BF),
             pltpu.VMEM((2, 2, 8, 64, width), BF),
             pltpu.VMEM((2, 2, 2, 2, 5, 64, width), BF),
             pltpu.VMEM((2, 2, 2, 64, width), BF),
@@ -709,7 +793,7 @@
             dma((5,)), dma((5,)),
             dma((2, 2)), dma((2, 2)), dma((2, 2)), dma((2, 2)),
             dma((2, 2, 2, 2)), dma((2, 2, 2, 6)),
-            dma((2, 2)), dma((2, 2)), dma((2, 2)), dma((2, 2, 3)), dma((2, 2)), dma((2, 2, 4)),
+            dma((2, 4)), dma((2, 4)), dma((2, 4)), dma((2, 4, 3)), dma((2, 4)), dma((2, 4, 4)),
             dma((2, 2, 2, 2)), dma((2, 2, 2, 6)), dma((2, 2)), dma((2, 2)), dma((2, 2)), dma((2, 2)),
         ],
         compiler_params=pltpu.CompilerParams(
@@ -723,15 +807,16 @@
         in_specs=[hbm] * 4 + [vmem] * 3,
         out_specs=(hbm, hbm, vmem, hbm, hbm, hbm),
         scratch_shapes=[
-            pltpu.VMEM((128, model_width), BF),
+            pltpu.VMEM((2, 8, 32, width), BF),
             pltpu.VMEM((width, hidden), BF),
             pltpu.VMEM((width, hidden), BF),
             pltpu.VMEM((hidden, width), BF),
             pltpu.VMEM((128, model_width), BF),
-            dma((7,)), dma((7,)), dma((8,)),
+            pltpu.VMEM((128, model_width), BF),
+            dma((2, 2)), dma((3,)), dma((3,)), dma((2, 4)),
         ],
         compiler_params=pltpu.CompilerParams(vmem_limit_bytes=60 * 1024 * 1024),
-    )(mixed, ggrad, ugrad, dgrad, back, select, pgrad)
+    )(eo, ggrad, ugrad, dgrad, split, select, pgrad)
     return mixed, igrad, pgrad.T, ggrad, ugrad, dgrad
 
 

time: 157 us -> 154 us (0.981)
  Pallas kernels: 157 us -> 153 us
    pallas_call x1, Pallas kernels: 150 us -> 147 us  [on_device(): pl.pallas_call(functools.partial(kernel, width), out_shape=(jax.ShapeDtyp...]
where the time goes in v4:
time: 154 us
  Pallas kernels  153 us (99%)
    pallas_call x1, Pallas kernels, on_device(): pl.pallas_call(functools.partial(kernel, width), out_shape=(jax.ShapeDtyp...  147 us
    pallas_call x1, Pallas kernels, on_device(): pl.pallas_call(functools.partial(finish, width), out_shape=(row_shape, ro...  5.6 us

profile of v4, /device:TPU:1, one launch (start us, length us, event | category | flops | bytes accessed | tf_op | source)
XLA Modules:
  0.0 153.9 jit_solution(4252491078127256613)
XLA Ops:
  0.6 147.4 %shard_map.127 = (bf16[128,128]{1,0:T(8,128)(2,1)}, f32[8,128]{1,0:T(8,128)}, bf16[896,512]{1,0:T(8,128)(2,1)}, bf16[896,512]{1,0:T(8,128)(2,1)}, bf16[512,896]{...) custom-call(s32[8,128]{1,0:T(8,128)} %bitcast.3, f32[8,128]{1,0:T(8,128)} %bitcast.4, ...), custom_call_target="tpu_custom_call" | custom-call | flops 8455716864 | bytes 16000000 | tf_op jit(solution)/shard_map/pallas_call | solution.py:756
  148.1 5.6 %shard_map.128 = (bf16[128,7168]{1,0:T(8,128)(2,1)}, bf16[128,7168]{1,0:T(8,128)(2,1)}, f32[8,128]{1,0:T(8,128)}, bf16[896,512]{1,0:T(8,128)(2,1)}, bf16[896,512]{1,0:T(8,128)(2,1)}, /*index=5*/bf16[512,896]{1,0:T(8,128)(2,1)}) custom-call(bf16[2,8,32,896]{3,2,1,0:T(8,128)(2,1)} %get-tuple-element.19.eo_in, bf16[896,512]{1,0:T(8,128)(2,1)} %get-tuple-element.20.ggrad_in, ...), custom_call_target="tpu_custom_call" | custom-call | tf_op jit(solution)/shard_map/pallas_call | solution.py:804

commit v5 on v4

--- a/solution.py
+++ b/solution.py
@@ -183,17 +183,18 @@
     def is_one(p):
         return is_zero(lax.rem(p + 7, 8))
 
-    def z_send(arr, q, d, half, p, s):
+    def z_send(arr, q, d, half, p, s, piece):
+        rows = pl.ds(32 * piece, 32)
         there = slot_of(d, s + 1)
         if s == 0:
             first = is_zero(p)
             slot = there + first * (8 + d - there)
-            rcopy(zsrc.at[arr, q, half], tokin.at[arr, q, slot], zs_s.at[arr, q, d, half], zs_r.at[arr, q, d, 1 - first], z_dev(d, False)).start()
+            rcopy(zsrc.at[arr, q, half, rows], tokin.at[arr, q, slot, rows], zs_s.at[arr, q, d, half], zs_r.at[arr, q, d, 1 - first, piece], z_dev(d, False)).start()
         else:
             came = slot_of(d, s)
             if s == 1:
                 came = came + is_one(p) * (8 + d - came)
-            rcopy(tokin.at[arr, q, came], tokin.at[arr, q, there], zs_s.at[arr, q, d, half], zs_r.at[arr, q, d, s + 1], z_dev(d, False)).start()
+            rcopy(tokin.at[arr, q, came, rows], tokin.at[arr, q, there, rows], zs_s.at[arr, q, d, half], zs_r.at[arr, q, d, s + 1, piece], z_dev(d, False)).start()
 
     def z_sent(arr, q):
         for d in (R, L):
@@ -216,12 +217,13 @@
                 if s == 1:
                     transit = is_one(p)
                     slot = slot + transit * (8 + d - slot)
-                wait_in(tokin.at[arr, q, slot], zs_r.at[arr, q, d, s * (1 - transit)])
-                if s < 5:
-
-                    @pl.when(p <= 4)
-                    def _():
-                        z_send(arr, q, d, half, p, s)
+                for piece in (0, 1):
+                    wait_in(tokin.at[arr, q, slot, pl.ds(32 * piece, 32)], zs_r.at[arr, q, d, s * (1 - transit), piece])
+                    if s < 5:
+
+                        @pl.when(p <= 4)
+                        def _():
+                            z_send(arr, q, d, half, p, s, piece)
 
         each_half(d, body)
 
@@ -231,7 +233,8 @@
             def body(half, p):
                 @pl.when(p < 4 if far else p == 4)
                 def _():
-                    z_send(arr, q, d, half, p, 0)
+                    z_send(arr, q, d, half, p, 0, 0)
+                    z_send(arr, q, d, half, p, 0, 1)
 
             each_half(d, body)
 
@@ -371,12 +374,13 @@
             piece = piece + lax.dot_general(acts[2, m].reshape(256, 512), wu[...], NT, preferred_element_type=F32)
         outp[arr, q, pl.ds(4 * part_of, 4)] = piece.astype(BF).reshape(4, 64, width)
 
-    def zb_copy(arr, q, d, half, p, s, whole):
-        src = outp.at[arr, q, slot_of(d, s)] if whole else rbuf.at[arr, q, d, half, s]
+    def zb_copy(arr, q, d, half, p, s, whole, piece):
+        rows = pl.ds(32 * piece, 32)
+        src = outp.at[arr, q, slot_of(d, s), rows] if whole else rbuf.at[arr, q, d, half, s, rows]
         sem = s - 1
         if s == 1:
             sem = 5 * is_one(p)
-        return rcopy(src, rbuf.at[arr, q, d, half, s - 1], zb_s.at[arr, q, d, half], zb_r.at[arr, q, d, sem], z_dev(d, True))
+        return rcopy(src, rbuf.at[arr, q, d, half, s - 1, rows], zb_s.at[arr, q, d, half], zb_r.at[arr, q, d, sem, piece], z_dev(d, True))
 
     def zb_begin(arr, q):
         for d in (R, L):
@@ -385,7 +389,8 @@
                 @pl.when(p == 5)
                 def _():
                     for s in (5, 4, 3, 2, 1):
-                        zb_copy(arr, q, d, half, p, s, True).start()
+                        for piece in (0, 1):
+                            zb_copy(arr, q, d, half, p, s, True, piece).start()
 
             each_half(d, body)
 
@@ -396,15 +401,17 @@
                 sem = s
                 if s == 0:
                     sem = 5 * is_zero(p)
-                wait_in(rbuf.at[arr, q, d, half, s], zb_r.at[arr, q, d, sem])
-                if s > 0:
-
-                    @pl.when(p >= 2)
-                    def _():
-                        total = rbuf[arr, q, d, half, s].astype(F32) + outp[arr, q, slot_of(d, s)].astype(F32)
-                        rbuf[arr, q, d, half, s] = total.astype(BF)
-
-                    zb_copy(arr, q, d, half, p, s, False).start()
+                for piece in (0, 1):
+                    rows = pl.ds(32 * piece, 32)
+                    wait_in(rbuf.at[arr, q, d, half, s, rows], zb_r.at[arr, q, d, sem, piece])
+                    if s > 0:
+
+                        @pl.when(p >= 2)
+                        def _():
+                            total = rbuf[arr, q, d, half, s, rows].astype(F32) + outp[arr, q, slot_of(d, s), rows].astype(F32)
+                            rbuf[arr, q, d, half, s, rows] = total.astype(BF)
+
+                        zb_copy(arr, q, d, half, p, s, False, piece).start()
 
         each_half(d, body)
 
@@ -792,9 +799,9 @@
             pltpu.VMEM((128, 128), BF),
             dma((5,)), dma((5,)),
             dma((2, 2)), dma((2, 2)), dma((2, 2)), dma((2, 2)),
-            dma((2, 2, 2, 2)), dma((2, 2, 2, 6)),
+            dma((2, 2, 2, 2)), dma((2, 2, 2, 6, 2)),
             dma((2, 4)), dma((2, 4)), dma((2, 4)), dma((2, 4, 3)), dma((2, 4)), dma((2, 4, 4)),
-            dma((2, 2, 2, 2)), dma((2, 2, 2, 6)), dma((2, 2)), dma((2, 2)), dma((2, 2)), dma((2, 2)),
+            dma((2, 2, 2, 2)), dma((2, 2, 2, 6, 2)), dma((2, 2)), dma((2, 2)), dma((2, 2)), dma((2, 2)),
         ],
         compiler_params=pltpu.CompilerParams(
             collective_id=0, has_side_effects=True, vmem_limit_bytes=60 * 1024 * 1024

time: 154 us -> 153 us (level)
  no operation moved by 1% of the time
where the time goes in v5:
time: 153 us
  Pallas kernels  152 us (99%)
    pallas_call x1, Pallas kernels, on_device(): pl.pallas_call(functools.partial(kernel, width), out_shape=(jax.ShapeDtyp...  147 us
    pallas_call x1, Pallas kernels, on_device(): pl.pallas_call(functools.partial(finish, width), out_shape=(row_shape, ro...  5.6 us

profile of v5, /device:TPU:1, one launch (start us, length us, event | category | flops | bytes accessed | tf_op | source)
XLA Modules:
  0.0 153.1 jit_solution(18399181101440288785)
XLA Ops:
  0.6 146.6 %shard_map.127 = (bf16[128,128]{1,0:T(8,128)(2,1)}, f32[8,128]{1,0:T(8,128)}, bf16[896,512]{1,0:T(8,128)(2,1)}, bf16[896,512]{1,0:T(8,128)(2,1)}, bf16[512,896]{...) custom-call(s32[8,128]{1,0:T(8,128)} %bitcast.3, f32[8,128]{1,0:T(8,128)} %bitcast.4, ...), custom_call_target="tpu_custom_call" | custom-call | flops 8455716864 | bytes 16000000 | tf_op jit(solution)/shard_map/pallas_call | solution.py:763
  147.3 5.6 %shard_map.128 = (bf16[128,7168]{1,0:T(8,128)(2,1)}, bf16[128,7168]{1,0:T(8,128)(2,1)}, f32[8,128]{1,0:T(8,128)}, bf16[896,512]{1,0:T(8,128)(2,1)}, bf16[896,512]{1,0:T(8,128)(2,1)}, /*index=5*/bf16[512,896]{1,0:T(8,128)(2,1)}) custom-call(bf16[2,8,32,896]{3,2,1,0:T(8,128)(2,1)} %get-tuple-element.19.eo_in, bf16[896,512]{1,0:T(8,128)(2,1)} %get-tuple-element.20.ggrad_in, ...), custom_call_target="tpu_custom_call" | custom-call | tf_op jit(solution)/shard_map/pallas_call | solution.py:811
